TPU v7x, 128 devices: a whole 4x4x4 slice. The times are simulated.
128 devices in a mesh: seq: 16 (over z, x), exp: 8 (over y, core).
Axes of the slice: x: 4, y: 4, z: 4, core: 2. Of those that a mesh axis runs over, the one named last changes fastest.
Arguments:
- queries: bfloat16 [3, 2048, 4096], P(None, 'seq', 'exp'), may hold values from -6 to 6
- key_rows: bfloat16 [3, 2048, 1024], P(None, 'seq', 'exp'), may hold values from -6 to 6
- value_rows: bfloat16 [3, 2048, 1024], P(None, 'seq', 'exp'), may hold values from -6 to 6
- residual: bfloat16 [3, 2048, 4096], P(None, ('seq', 'exp')), may hold values from -6 to 6
- w_out: bfloat16 [4096, 4096], P('exp'), may hold values from -3 to 3
- norm_gain: float32 [4096], replicated, may hold values from 0.1 to 1.9
- w_gate: bfloat16 [128, 4096, 768], P(('seq', 'exp')), may hold values from -0.09375 to 0.09375
- w_up: bfloat16 [128, 4096, 768], P(('seq', 'exp')), may hold values from -0.09375 to 0.09375
- w_down: bfloat16 [128, 768, 4096], P(('seq', 'exp')), may hold values from -0.21875 to 0.21875
- routes: int32 [2048, 8], P(('seq', 'exp')), may hold values from 0 to 63, all different within a row; in each aligned block of 16 rows (0 to 15, 16 to 31, ...) at most 3 rows name the same one
- route_gain: float32 [2048, 8], P(('seq', 'exp')), may hold values from 0.03 to 0.3
Outputs:
- layer_out: bfloat16 [3, 2048, 4096], P(None, ('seq', 'exp'))
- probe_products: float32 [2, 2048], P(None, ('seq', 'exp'))
Inputs may be any that keep to these rules, and one draw needn't show every extreme that they name: `routes`: each row names 8 different experts; among the 16 rows of one device no expert is named more than 3 times, and in some device's rows some expert is named exactly 3 times.
All inputs are finite; a program needn't handle non-finite values.
Results may differ from a plain program's by a relative error of at most 0.023.
Values may be sent and summed in bfloat16 or wider, within the bound.
A program may use at most 192 MiB of HBM per device.

v0:
```python
import math

import jax
import jax.numpy as jnp
from jax import lax
from jax.sharding import PartitionSpec as P

HEADS = 32
KVH = 8
HD = 128


EPS = 1e-06


def shards(
    queries,
    key_rows,
    value_rows,
    residual,
    w_out,
    norm_gain,
    w_gate,
    w_up,
    w_down,
    routes,
    route_gain,
):
    streams, seq_local, q_width = queries.shape
    kv_local = key_rows.shape[2] // HD
    groups = HEADS // KVH
    score_scale = 1.0 / math.sqrt(HD)
    queries_split = queries.reshape(streams, seq_local, kv_local, groups, HD)
    image_length = lax.axis_size("seq") * seq_local
    my_image = lax.axis_index("seq") * seq_local // image_length
    highest = lax.Precision.HIGHEST
    stat_shape = (kv_local, groups, seq_local)
    start_state = (
        jnp.full(stat_shape, -1e30, jnp.float32),
        jnp.zeros(stat_shape, jnp.float32),
        jnp.zeros(stat_shape + (HD,), jnp.float32),
        jnp.zeros((2,) + stat_shape + (HD,), jnp.float32),
        jnp.zeros((2,) + stat_shape, jnp.float32),
        jnp.zeros((2,) + stat_shape + (HD,), jnp.float32),
    )
    key_piece = lax.all_gather(key_rows, "seq", axis=1, tiled=True)
    value_piece = lax.all_gather(value_rows, "seq", axis=1, tiled=True)
    width = key_piece.shape[1]
    key_piece = key_piece.reshape(streams, width, kv_local, HD)
    value_float = value_piece.reshape(streams, width, kv_local, HD).astype(jnp.float32)
    scores = (
        jnp.einsum(
            "qkgd,nkd->kgqn", queries_split[0], key_piece[0], preferred_element_type=jnp.float32
        )
        * score_scale
    )
    slope_list = []
    for probe in (1, 2):
        left_term = jnp.einsum(
            "qkgd,nkd->kgqn", queries_split[probe], key_piece[0], preferred_element_type=jnp.float32
        )
        right_term = jnp.einsum(
            "qkgd,nkd->kgqn", queries_split[0], key_piece[probe], preferred_element_type=jnp.float32
        )
        slope_list.append((left_term + right_term) * score_scale)
    slopes = jnp.stack(slope_list)
    key_pos = jnp.arange(width)
    valid = key_pos // image_length == my_image
    run_max, run_sum, acc_main, acc_values, acc_slopes, acc_mixed = start_state
    new_max = jnp.maximum(run_max, jnp.max(jnp.where(valid, scores, -1e30), axis=-1))
    weights = jnp.where(valid, jnp.exp(scores - new_max[..., None]), 0.0)
    run_sum = jnp.sum(weights, axis=-1)
    acc_main = jnp.einsum("kgqn,nkd->kgqd", weights, value_float[0], precision=highest)
    acc_values = jnp.einsum("kgqn,snkd->skgqd", weights, value_float[1:], precision=highest)
    weighted_slopes = weights[None] * slopes
    acc_slopes = jnp.sum(weighted_slopes, axis=-1)
    acc_mixed = jnp.einsum("skgqn,nkd->skgqd", weighted_slopes, value_float[0], precision=highest)
    final_state = (new_max, run_sum, acc_main, acc_values, acc_slopes, acc_mixed)
    run_max, run_sum, acc_main, acc_values, acc_slopes, acc_mixed = final_state
    main_out = acc_main / run_sum[..., None]
    tangent_out = (acc_mixed + acc_values) / run_sum[None, ..., None] - (
        acc_slopes / run_sum[None]
    )[..., None] * main_out[None]
    all_out = jnp.concatenate([main_out[None], tangent_out], axis=0)
    attended = (
        all_out.transpose(0, 3, 1, 2, 4).reshape(streams, seq_local, q_width).astype(jnp.bfloat16)
    )
    tok_local = routes.shape[0]
    head_part = lax.psum_scatter(
        jnp.einsum("sqh,hd->qsd", attended, w_out, preferred_element_type=jnp.float32).astype(
            jnp.bfloat16
        ),
        "exp",
        scatter_dimension=0,
        tiled=True,
    ).astype(jnp.float32)
    summed = residual.astype(jnp.float32).transpose(1, 0, 2) + head_part
    main_sum = summed[:, 0]
    recip = lax.rsqrt(jnp.mean(main_sum * main_sum, axis=-1, keepdims=True) + EPS)
    main_norm = main_sum * recip * norm_gain
    inner = jnp.mean(main_sum[:, None, :] * summed[:, 1:], axis=-1, keepdims=True)
    recip_wide = recip[:, None, :]
    tangent_norm = (
        summed[:, 1:] * recip_wide
        - main_sum[:, None, :] * (recip_wide * recip_wide * recip_wide) * inner
    ) * norm_gain
    normed = jnp.concatenate([main_norm[:, None], tangent_norm], axis=1).astype(jnp.bfloat16)
    top_count = routes.shape[1]
    experts_all = w_gate.shape[0] * lax.axis_size(("seq", "exp")) // 2
    slot_room = 3 * tok_local * top_count // (2 * experts_all)
    flat_routes = routes.reshape(-1)
    one_hot = (flat_routes[:, None] == jnp.arange(experts_all)[None, :]).astype(jnp.int32)
    running_count = jnp.cumsum(one_hot, axis=0)
    slot_of = jnp.sum(one_hot * running_count, axis=1) - 1
    token_of = jnp.arange(tok_local * top_count) // top_count
    width_model = normed.shape[2]
    send_once = jnp.zeros((experts_all, slot_room, streams, width_model), jnp.bfloat16)
    send_once = send_once.at[flat_routes, slot_of].set(normed[token_of])
    send_both = jnp.broadcast_to(
        send_once[:, None], (experts_all, 2, slot_room, streams, width_model)
    )
    send_both = send_both.reshape(2 * experts_all, slot_room, streams, width_model)
    arrived = lax.all_to_all(send_both, ("seq", "exp"), split_axis=0, concat_axis=0, tiled=True)
    senders = arrived.shape[0]
    slots_here = arrived.shape[1]
    flat_rows = arrived.reshape(senders * slots_here, streams, width_model)
    gate_pre = jnp.einsum("rsd,df->rsf", flat_rows, w_gate[0], preferred_element_type=jnp.float32)
    up_pre = jnp.einsum("rsd,df->rsf", flat_rows, w_up[0], preferred_element_type=jnp.float32)
    sigma = jax.nn.sigmoid(gate_pre[:, 0])
    activ = gate_pre[:, 0] * sigma
    slope = sigma * (1.0 + gate_pre[:, 0] * (1.0 - sigma))
    main_hidden = activ * up_pre[:, 0]
    tangent_hidden = (
        slope[:, None] * gate_pre[:, 1:] * up_pre[:, 0][:, None] + activ[:, None] * up_pre[:, 1:]
    )
    hidden = jnp.concatenate([main_hidden[:, None], tangent_hidden], axis=1).astype(jnp.bfloat16)
    outputs = jnp.einsum(
        "rsf,fd->rsd", hidden, w_down[0], preferred_element_type=jnp.float32
    ).astype(jnp.bfloat16)
    produced = outputs.reshape(senders, slots_here, streams, width_model)
    came_back = lax.all_to_all(produced, ("seq", "exp"), split_axis=0, concat_axis=0, tiled=True)
    merged = (
        came_back.astype(jnp.float32)
        .reshape(experts_all, 2, slot_room, streams, width_model)
        .sum(axis=1)
    )
    merged = merged.reshape(experts_all * slot_room, streams, width_model)
    picked = merged[flat_routes * slot_room + slot_of].reshape(
        tok_local, top_count, streams, width_model
    )
    expert_sum = jnp.sum(picked * route_gain[:, :, None, None], axis=1)
    combined = summed + expert_sum
    combined_streams = combined.transpose(1, 0, 2)
    layer_out = combined_streams.astype(jnp.bfloat16)
    probe_products = jnp.mean(residual[1:].astype(jnp.float32) * combined_streams[1:], axis=-1)
    return (layer_out, probe_products)


def solution(mesh):
    return jax.shard_map(
        shards,
        mesh=mesh,
        in_specs=(
            P(None, "seq", "exp"),
            P(None, "seq", "exp"),
            P(None, "seq", "exp"),
            P(None, ("seq", "exp"), None),
            P("exp", None),
            P(),
            P(("seq", "exp"), None, None),
            P(("seq", "exp"), None, None),
            P(("seq", "exp"), None, None),
            P(("seq", "exp"), None),
            P(("seq", "exp"), None),
        ),
        out_specs=(P(None, ("seq", "exp"), None), P(None, ("seq", "exp"))),
        check_vma=False,
    )
```

profile of v0, /device:TPU:2, one launch (start us, length us, event | category | flops | bytes accessed | tf_op | source)
XLA Modules:
  0.0 667.9 jit_solution(15453927465876010100)
XLA Ops:
  11.1 45.1 %all-gather.3.cloned.1.call-done = bf16[3,2048,128]{2,1,0:T(8,128)(2,1)} async-done(((bf16[3,128,128]{2,1,0:T(8,128)(2,1)}), bf16[3,2048,128]{2,1,0:T(8,128)(2,1)}) %all-gather.3.cloned.1.call-update) | async-done | bytes 1572880 | tf_op jit(solution)/shard_map/all_gather | solution.py:46
  62.5 41.3 %all-gather.5.cloned.1.call-done = bf16[3,2048,128]{1,2,0:T(8,128)(2,1)} async-done(((bf16[3,128,128]{1,2,0:T(8,128)(2,1)}), bf16[3,2048,128]{1,2,0:T(8,128)(2,1)}) %all-gather.5.cloned.1.call-update) | async-done | bytes 1572880 | tf_op jit(solution)/shard_map/all_gather | solution.py:47
  103.8 3.8 convolution_divide_fusion
  120.9 3.5 fusion.9
  125.1 34.7 %reduce-scatter.2.cloned.1.call-done = bf16[16,3,4096]{2,0,1:T(8,128)(2,1)} async-done(((bf16[128,3,4096]{2,0,1:T(8,128)(2,1)}), bf16[16,3,4096]{2,0,1:T(8,128)(2,1)}) %reduce-scatter.2.cloned.1.call-update) | async-done | bytes 393232 | tf_op jit(solution)/shard_map/reduce_scatter | solution.py:89
  161.9 7.8 %gather_fusion = bf16[128,3,4096]{2,1,0:T(4,128)(2,1)} fusion(bf16[16,3,4096]{2,1,0:T(4,128)(2,1)S(1)} %copy.104, s32[1024]{0:T(1024)S(1)} %pad_clamp_fusion.1), kind=kCustom, calls=%fused_computation | custom fusion | bytes 6291968 | tf_op jit(solution)/shard_map/gather | solution.py:118
  169.7 5.8 broadcast_in_dim.26
  175.5 21.0 %scatter_fusion = bf16[64,3,3,4096]{3,2,1,0:T(4,128)(2,1)} fusion(bf16[64,3,3,4096]{3,2,1,0:T(4,128)(2,1)} %broadcast_in_dim.26, s32[128]{0:T(128)S(1)} %get-tuple-element.17, bf16[128,3,4096]{2,1,0:T(4,128)(2,1)} %gather_fusion), kind=kCustom, calls=%fused_computation.2 | custom fusion | bytes 9438208 | tf_op jit(solution)/shard_map/scatter | solution.py:118
  196.6 8.8 %copy.105 = bf16[64,3,3,4096]{3,1,2,0:T(4,128)(2,1)S(1)} copy(bf16[64,3,3,4096]{3,2,1,0:T(4,128)(2,1)} %scatter_fusion) | data formatting | bytes 9437184 | tf_op jit(solution)/shard_map/scatter | solution.py:118
  205.4 6.0 broadcast_in_dim.27
  211.4 149.5 %all_to_all.10 = bf16[128,3,3,4096]{3,1,2,0:T(4,128)(2,1)S(1)} all-to-all(bf16[128,3,3,4096]{3,1,2,0:T(4,128)(2,1)S(1)} %bitcast.176), channel_id=1, replica_groups=mesh['seq'=16,'exp'=8] {'seq','exp'}, dimensions={0} | all-to-all | bytes 18874368 | tf_op jit(solution)/shard_map/all_to_all | solution.py:123
  360.9 6.2 copy.106
  367.1 20.1 %reshape.362 = bf16[384,3,4096]{2,0,1:T(8,128)(2,1)} reshape(bf16[128,3,3,4096]{3,1,0,2:T(4,128)(2,1)} %copy.106) | data formatting | bytes 18874368 | tf_op jit(solution)/shard_map/reshape | solution.py:126
  387.2 12.0 %fusion.5 = f32[384,3,768]{2,0,1:T(8,128)S(1)} fusion(bf16[384,3,4096]{2,0,1:T(8,128)(2,1)} %reshape.362, bf16[1,4096,768]{2,1,0:T(8,128)(2,1)} %param.18), kind=kOutput, calls=%fused_computation.13 | convolution fusion | flops 7247757312 | bytes 19267584 | tf_op jit(solution)/shard_map/rsd,df->rsf/dot_general | solution.py:128
  399.3 7.6 %fusion.7 = f32[384,3,768]{2,0,1:T(8,128)S(1)} fusion(bf16[384,3,4096]{2,0,1:T(8,128)(2,1)S(1)} %copy-done.3, bf16[1,4096,768]{2,1,0:T(8,128)(2,1)S(1)} %bitcast.192), kind=kOutput, calls=%fused_computation.15 | convolution fusion | flops 7247757312 | bytes 19267584 | tf_op jit(solution)/shard_map/rsd,df->rsf/dot_general | solution.py:127
  409.9 9.9 %convolution_convert_fusion = bf16[384,3,4096]{2,0,1:T(8,128)(2,1)} fusion(bf16[1,768,4096]{2,1,0:T(8,128)(2,1)S(1)} %bitcast.194, bf16[384,2,768]{2,0,1:T(8,128)(2,1)S(1)} %fusion.18, bf16[384,1,768]{2,0,1:T(8,128)(2,1)S(1)} %get-tuple-element.6), kind=kOutput, calls=%fused_computation.11 | convolution fusion | flops 7253360640 | bytes 17498112 | tf_op jit(solution)/shard_map/rsf,fd->rsd/dot_general | solution.py:137
  419.8 18.7 %reshape.363 = bf16[128,3,3,4096]{3,1,0,2:T(4,128)(2,1)} reshape(bf16[384,3,4096]{2,0,1:T(8,128)(2,1)} %convolution_convert_fusion) | data formatting | bytes 18874368 | tf_op jit(solution)/shard_map/reshape | solution.py:140
  438.5 11.5 %copy.107 = bf16[128,3,3,4096]{3,1,2,0:T(4,128)(2,1)} copy(bf16[128,3,3,4096]{3,1,0,2:T(4,128)(2,1)} %reshape.363) | data formatting | bytes 18874368 | tf_op jit(solution)/shard_map/reshape | solution.py:140
  450.0 6.3 all-to-all-start.1
  456.4 153.4 %all-to-all-done.1 = bf16[128,3,3,4096]{3,1,2,0:T(4,128)(2,1)} async-done(((bf16[128,3,3,4096]{3,1,2,0:T(4,128)(2,1)}), bf16[128,3,3,4096]{3,1,2,0:T(4,128)(2,1)}, u32[]{:S(2)}, u32[]{:S(2)}) %all-to-all-start.1) | async-done | bytes 9437216 | tf_op jit(solution)/shard_map/all_to_all | solution.py:141
  609.7 15.4 %convert_reduce_fusion = f32[64,3,3,4096]{3,1,2,0:T(4,128)S(1)} fusion(bf16[128,3,3,4096]{3,1,2,0:T(4,128)(2,1)} %all-to-all-done.1), kind=kLoop, calls=%fused_computation.3 | loop fusion | flops 7077888 | bytes 18874368 | tf_op jit(solution)/shard_map/reduce_sum | solution.py:145
  625.2 13.4 %copy.124 = f32[64,3,3,4096]{3,2,1,0:T(4,128)} copy(f32[64,3,3,4096]{3,1,2,0:T(4,128)S(1)} %convert_reduce_fusion) | data formatting | bytes 18874368 | tf_op jit(solution)/shard_map/reshape | solution.py:147
  638.5 14.1 %gather_fusion.1 = f32[128,3,4096]{2,1,0:T(4,128)} fusion(f32[192,3,4096]{2,1,0:T(4,128)} %bitcast.181, s32[1024]{0:T(1024)S(1)} %pad_clamp_fusion), kind=kCustom, calls=%fused_computation.1 | custom fusion | bytes 12583424 | tf_op jit(solution)/shard_map/gather | solution.py:148
  652.7 6.4 multiply_reduce_fusion
  (85 shorter events, 31.1 us)
Async XLA Ops:
  7.2 49.1 %all-gather.3.cloned.1.call-start = ((), (), s32[]{:S(2)}) async-start(), calls=%async_computation.3 | async-start | bytes 1671168 | tf_op jit(solution)/shard_map/all_gather | solution.py:46
  7.9 95.9 %all-gather.5.cloned.1.call-start = ((), (), s32[]{:S(2)}) async-start(), calls=%async_computation.4 | async-start | bytes 1671168 | tf_op jit(solution)/shard_map/all_gather | solution.py:47
  9.6 150.2 %reduce-scatter.2.cloned.1.call-start = ((), (), s32[]{:S(2)}) async-start(), calls=%async_computation.5 | async-start | bytes 3538944 | tf_op jit(solution)/shard_map/reduce_scatter | solution.py:89
  58.1 1.9 copy-start.1
  62.5 45.2 %copy-start.4 = (bf16[3,2048,128]{2,1,0:T(8,128)(2,1)S(1)}, bf16[3,2048,128]{2,1,0:T(8,128)(2,1)}, u32[]{:S(2)}) copy-start(bf16[3,2048,128]{2,1,0:T(8,128)(2,1)} %all-gather.3.cloned.1.call-done) | copy-start | bytes 4718596
  109.7 2.2 copy-start
  111.9 2.2 copy-start.2
  111.9 2.7 copy-start.8
  117.5 3.3 copy-start.5
  120.9 3.5 copy-start.10
  120.9 39.0 %copy-start.6 = (bf16[3,16,4096]{2,1,0:T(8,128)(2,1)S(1)}, bf16[3,16,4096]{2,1,0:T(8,128)(2,1)}, u32[]{:S(2)}) copy-start(bf16[3,16,4096]{2,1,0:T(8,128)(2,1)} %param.14) | copy-start | bytes 1179652
  124.4 36.7 %copy-start.9 = (f32[4096]{0:T(1024)S(1)}, f32[4096]{0:T(1024)}, u32[]{:S(2)}) copy-start(f32[4096]{0:T(1024)} %param.16) | copy-start | bytes 49156
  367.1 32.1 %slice-start = ((s8[6291456]{0:T(1024)(128)(4,1)}), s8[2097152]{0:T(1024)(128)(4,1)S(1)}, s32[]{:S(2)}) async-start(s8[6291456]{0:T(1024)(128)(4,1)} %bitcast.191), calls=%async_computation.6 | async-start | bytes 4194304
  387.2 12.0 %copy-start.3 = (bf16[384,3,4096]{2,0,1:T(8,128)(2,1)S(1)}, bf16[384,3,4096]{2,0,1:T(8,128)(2,1)}, u32[]{:S(2)}) copy-start(bf16[384,3,4096]{2,0,1:T(8,128)(2,1)} %reshape.362) | copy-start | bytes 28311556
  387.2 12.0 %slice-start.1 = ((s8[6291456]{0:T(1024)(128)(4,1)}), s8[4194304]{0:T(1024)(128)(4,1)S(1)}, s32[]{:S(2)}) async-start(s8[6291456]{0:T(1024)(128)(4,1)} %bitcast.191), calls=%async_computation.7 | async-start | bytes 8388608
  406.9 2.2 slice-start.2
  407.4 2.5 slice-start.3
  450.0 6.3 copy-start.11
  450.0 159.8 %all-to-all-start.1 = ((bf16[128,3,3,4096]{3,1,2,0:T(4,128)(2,1)}), bf16[128,3,3,4096]{3,1,2,0:T(4,128)(2,1)}, u32[]{:S(2)}, u32[]{:S(2)}) async-start(bf16[128,3,3,4096]{3,1,2,0:T(4,128)(2,1)} %copy.107), calls=%async_computation.2 | async-start | bytes 25165824 | tf_op jit(solution)/shard_map/all_to_all | solution.py:141
  652.7 6.4 copy-start.7
Sparse Core Ops, SparseCore 0:
  10.1 46.0 all-gather.2
  58.9 44.8 all-gather.4
  124.5 35.2 reduce-scatter.1
where the time goes:
time: 678 us; the launch traced here: 668 us
  waiting for transfers between devices  275 us (41%)
  blocking collectives  150 us (22%)
  local copies, waits for them, and re-layouts  144 us (21%)
  matrix products  47.6 us (7%)
  other arithmetic  30.4 us (4%)
  between operations  14.4 us (2%)
    all_to_all x1, waiting for transfers between devices, shards(): lax.all_to_all(produced, ('seq', 'exp'), split_axis=0, concat_axis=0, til...  153 us
    all_to_all x1, blocking collectives, shards(): lax.all_to_all(send_both, ('seq', 'exp'), split_axis=0, concat_axis=0, ti...  150 us
    all_gather x1, waiting for transfers between devices, shards(): key_piece = lax.all_gather(key_rows, 'seq', axis=1, tiled=True)  45.1 us
    all_gather x1, waiting for transfers between devices, shards(): value_piece = lax.all_gather(value_rows, 'seq', axis=1, tiled=True)  41.3 us
    reduce_scatter x1, waiting for transfers between devices, shards(): lax.psum_scatter(jnp.einsum('sqh,hd->qsd', attended, w_out, preferred_ele...  34.7 us
    reshape x2, local copies, waits for them, and re-layouts, shards(): produced = outputs.reshape(senders, slots_here, streams, width_model)  30.2 us
    scatter x2, local copies, waits for them, and re-layouts, shards(): send_once = send_once.at[flat_routes, slot_of].set(normed[token_of])  29.9 us
    reshape x1, local copies, waits for them, and re-layouts, shards(): flat_rows = arrived.reshape(senders * slots_here, streams, width_model)  20.1 us
  transfers between devices with their start and end apart: 4, of which 4 were waited for; matrix products, arithmetic and copies ran while one was open for 1% of the time, Pallas kernels for 0%

commit v1 on v0

v1 whole, which is shorter than its diff:
```python
import math

import jax
import jax.numpy as jnp
from jax import lax
from jax.experimental import pallas as pl
from jax.experimental.pallas import tpu as pltpu
from jax.sharding import PartitionSpec as P

HD = 128
EPS = 1e-06
MESH = pl.DeviceIdType.MESH
BF = jnp.bfloat16
F32 = jnp.float32

SEQ = 16
KEYS = 128
TOK = 16
D = 4096
LANES = 256
FOLD = D // LANES
CHIPS = 64
SLOTS = 3
VECS = 3 * SLOTS
FH = 768
HALF = 32
ROWS = HALF * VECS
FT = 256
NT = 512


def dot(a, b):
    return jnp.dot(a, b, preferred_element_type=F32)


def dot_nt(a, b):
    return lax.dot_general(a, b, (((1,), (1,)), ((), ())), preferred_element_type=F32)


def attend_kernel(
    q_ref,
    k_ref,
    v_ref,
    res_ref,
    gain_ref,
    wo_ref,
    wg_ref,
    wu_ref,
    wd_ref,
    summed_ref,
    normed_ref,
    sg_ref,
    su_ref,
    sd_ref,
    kb,
    vb,
    qs,
    qc,
    scores,
    slopes,
    att,
    wo,
    sib_send,
    sib_recv,
    own,
    y_send,
    y_recv,
    stage,
    local_sem,
    w_send,
    w_recv,
    k_send,
    k_recv,
    v_send,
    v_recv,
    s_send,
    s_recv,
    ys_send,
    ys_recv,
):
    seq = lax.axis_index("seq")
    ex = lax.axis_index("exp")
    z, x = lax.div(seq, 4), lax.rem(seq, 4)
    y, core = lax.div(ex, 2), lax.rem(ex, 2)
    sibling = (seq, y * 2 + (1 - core))
    scale = 1.0 / math.sqrt(HD)

    def z_peer(d):
        return (lax.rem(z + d, 4) * 4 + x, ex)

    def x_peer(d):
        return (z * 4 + lax.rem(x + d, 4), ex)

    def y_peer(d):
        return (seq, lax.rem(y + d, 4) * 2 + core)

    wo_copy = pltpu.make_async_copy(wo_ref, wo, local_sem)
    wo_copy.start()

    barrier = pltpu.get_barrier_semaphore()
    pl.semaphore_signal(barrier, inc=1, device_id=sibling, device_id_type=MESH)
    for d in (1, 2, 3):
        for peer in (z_peer(d), x_peer(d), y_peer(d)):
            pl.semaphore_signal(barrier, inc=1, device_id=peer, device_id_type=MESH)
    kb[seq] = k_ref[...]
    vb[seq] = v_ref[...]
    pl.semaphore_wait(barrier, 10)

    def remote(src, dst, ssem, rsem, peer):
        return pltpu.make_async_remote_copy(
            src_ref=src, dst_ref=dst, send_sem=ssem, recv_sem=rsem, device_id=peer, device_id_type=MESH
        )

    def k_copy(origin, number, peer):
        return remote(kb.at[origin], kb.at[origin], k_send.at[number], k_recv.at[origin], peer)

    def v_copy(origin, number, peer):
        return remote(vb.at[origin], vb.at[origin], v_send.at[number], v_recv.at[origin], peer)

    order = (1, 3, 2)
    for d in order:
        k_copy(seq, d - 1, z_peer(d)).start()
        v_copy(seq, d - 1, x_peer(d)).start()
    for d in order:
        k_copy(seq, 3 + d - 1, x_peer(d)).start()
        v_copy(seq, 3 + d - 1, z_peer(d)).start()
    weight_copies = [
        remote(wg_ref, sg_ref, w_send.at[0], w_recv.at[0], sibling),
        remote(wu_ref, su_ref, w_send.at[1], w_recv.at[1], sibling),
        remote(wd_ref, sd_ref, w_send.at[2], w_recv.at[2], sibling),
    ]
    for copy in weight_copies:
        copy.start()

    for h in range(4):
        for s in range(3):
            qs[s, h * 128 : (h + 1) * 128, :] = q_ref[s, :, h * 128 : (h + 1) * 128]
    for t in (1, 2):
        qc[t - 1, :, :HD] = qs[t]
        qc[t - 1, :, HD:] = qs[0]

    for d in order:
        from_z = lax.rem(z + d, 4) * 4 + x
        from_x = z * 4 + lax.rem(x + d, 4)
        k_copy(from_z, 0, z_peer(d)).wait_recv()
        for e in order:
            k_copy(from_z, 3 * (d + 1) + e - 1, x_peer(e)).start()
        v_copy(from_x, 0, x_peer(d)).wait_recv()
        for e in order:
            v_copy(from_x, 3 * (d + 1) + e - 1, z_peer(e)).start()

    for dz in (0,) + order:
        c = lax.rem(z + dz, 4)
        for e in (1, 2, 3):
            k_copy(c * 4 + lax.rem(x + e, 4), 0, x_peer(e)).wait_recv()
        kc = kb[pl.ds(c * 4, 4)]
        k0 = kc[:, 0].reshape(512, HD)
        scores[c] = dot_nt(qs[0], k0) * scale
        for t in (1, 2):
            kt = kc[:, t].reshape(512, HD)
            slopes[t - 1, c] = dot_nt(qc[t - 1], jnp.concatenate([k0, kt], axis=1)) * scale

    for d in order:
        for e in (0, 1, 2, 3):
            origin = lax.rem(z + d, 4) * 4 + lax.rem(x + e, 4)
            v_copy(origin, 0, z_peer(d)).wait_recv()

    def head(h, carry):
        rows = pl.ds(pl.multiple_of(h * 128, 128), 128)
        top = jnp.max(scores[0, rows, :], axis=1, keepdims=True)
        for c in (1, 2, 3):
            top = jnp.maximum(top, jnp.max(scores[c, rows, :], axis=1, keepdims=True))
        total = jnp.zeros((128, 1), F32)
        r1 = jnp.zeros((128, 1), F32)
        r2 = jnp.zeros((128, 1), F32)
        acc = jnp.zeros((128, 3 * HD), F32)
        mixed = jnp.zeros((256, HD), F32)
        for c in range(4):
            p = jnp.exp(scores[c, rows, :] - top).astype(BF)
            pf = p.astype(F32)
            w1 = (pf * slopes[0, c, rows, :]).astype(BF)
            w2 = (pf * slopes[1, c, rows, :]).astype(BF)
            total += jnp.sum(pf, axis=1, keepdims=True)
            r1 += jnp.sum(w1.astype(F32), axis=1, keepdims=True)
            r2 += jnp.sum(w2.astype(F32), axis=1, keepdims=True)
            v0 = vb[4 * c : 4 * c + 4, 0].reshape(512, HD)
            v1 = vb[4 * c : 4 * c + 4, 1].reshape(512, HD)
            v2 = vb[4 * c : 4 * c + 4, 2].reshape(512, HD)
            acc += dot(p, jnp.concatenate([v0, v1, v2], axis=1))
            mixed += dot(jnp.concatenate([w1, w2], axis=0), v0)
        inv = 1.0 / total
        main = acc[:, :HD] * inv
        t1 = (mixed[:128] + acc[:, HD : 2 * HD]) * inv - (r1 * inv) * main
        t2 = (mixed[128:] + acc[:, 2 * HD :]) * inv - (r2 * inv) * main
        att[0, :, rows] = main.astype(BF)
        att[1, :, rows] = t1.astype(BF)
        att[2, :, rows] = t2.astype(BF)
        return carry

    lax.fori_loop(0, 4, head, 0)

    wo_copy.wait()

    def block_rows(parity):
        parts = []
        for d in range(4):
            j = lax.rem(y + d, 4) * 2 + parity
            rows = pl.ds(pl.multiple_of(j * TOK, TOK), TOK)
            for s in range(3):
                parts.append(att[s, rows, :])
        return jnp.concatenate(parts, axis=0)

    sib_rows = block_rows(1 - core)
    sib_copies = []
    for n in range(4):
        sib_send[n] = dot(sib_rows, wo[:, n * 1024 : (n + 1) * 1024]).astype(BF)
        copy = remote(sib_send.at[n], sib_recv.at[n], s_send.at[n], s_recv.at[n], sibling)
        copy.start()
        sib_copies.append(copy)
    own_rows = block_rows(core)
    y_copies = []
    for n in range(4):
        lanes = slice(n * 1024, (n + 1) * 1024)
        product = dot(own_rows, wo[:, lanes])
        sib_copies[n].wait_recv()
        both = product + sib_recv[n].astype(F32)
        own[:, lanes] = both[:48]
        for d in order:
            y_send[n, d - 1] = both[48 * d : 48 * (d + 1)].astype(BF)
            copy = remote(
                y_send.at[n, d - 1], y_recv.at[n, d - 1], ys_send.at[n, d - 1], ys_recv.at[n, d - 1], y_peer(d)
            )
            copy.start()
            y_copies.append(copy)
    for n in range(4):
        for d in (1, 2, 3):
            y_copies[n * 3 + order.index(d)].wait_recv()
        lanes = slice(n * 1024, (n + 1) * 1024)
        part = own[:, lanes]
        for d in (1, 2, 3):
            part += y_recv[n, d - 1].astype(F32)
        for s in range(3):
            summed_ref[s, :, lanes] = part[16 * s : 16 * (s + 1)] + res_ref[s, :, lanes].astype(F32)

    main_sum = summed_ref[0]
    recip = lax.rsqrt(jnp.mean(main_sum * main_sum, axis=-1, keepdims=True) + EPS)
    normed_ref[TOK] = jnp.zeros((3, FOLD, LANES), BF)
    for s in range(3):
        if s == 0:
            rows = main_sum * recip * gain_ref[...]
        else:
            inner = jnp.mean(main_sum * summed_ref[s], axis=-1, keepdims=True)
            rows = (summed_ref[s] * recip - main_sum * (recip * recip * recip * inner)) * gain_ref[...]
        for c in range(FOLD):
            for half in (0, 128):
                first = c * LANES + half
                stage[half // 128, pl.ds(c, TOK, stride=FOLD), :] = rows[:, first : first + 128]
        for half in (0, 1):
            normed_ref[:TOK, s, :, half * 128 : half * 128 + 128] = (
                stage[half].reshape(TOK, FOLD, 128).astype(BF)
            )

    for d in order:
        k_copy(seq, d - 1, z_peer(d)).wait_send()
        v_copy(seq, d - 1, x_peer(d)).wait_send()
    for number in range(3, 15):
        k_copy(seq, number, x_peer(1)).wait_send()
        v_copy(seq, number, z_peer(1)).wait_send()
    for copy in sib_copies + y_copies:
        copy.wait_send()
    for copy in weight_copies:
        copy.wait()


def attend(q, k, v, residual, gain, w_out, w_gate, w_up, w_down):
    vmem = pl.BlockSpec(memory_space=pltpu.VMEM)
    anywhere = pl.BlockSpec(memory_space=pl.ANY)
    dma = pltpu.SemaphoreType.DMA
    return pl.pallas_call(
        attend_kernel,
        out_shape=(
            jax.ShapeDtypeStruct((3, TOK, D), F32),
            jax.ShapeDtypeStruct((TOK + 1, 3, FOLD, LANES), BF),
            jax.ShapeDtypeStruct(w_gate.shape, BF),
            jax.ShapeDtypeStruct(w_up.shape, BF),
            jax.ShapeDtypeStruct(w_down.shape, BF),
        ),
        in_specs=[vmem] * 5 + [anywhere] * 4,
        out_specs=(vmem, vmem, anywhere, anywhere, anywhere),
        scratch_shapes=[
            pltpu.VMEM((SEQ, 3, KEYS, HD), BF),
            pltpu.VMEM((SEQ, 3, KEYS, HD), BF),
            pltpu.VMEM((3, 512, HD), BF),
            pltpu.VMEM((2, 512, 2 * HD), BF),
            pltpu.VMEM((4, 512, 512), F32),
            pltpu.VMEM((2, 4, 512, 512), F32),
            pltpu.VMEM((3, KEYS, 512), BF),
            pltpu.VMEM((512, D), BF),
            pltpu.VMEM((4, 192, 1024), BF),
            pltpu.VMEM((4, 192, 1024), BF),
            pltpu.VMEM((48, D), F32),
            pltpu.VMEM((4, 3, 48, 1024), BF),
            pltpu.VMEM((4, 3, 48, 1024), BF),
            pltpu.VMEM((2, TOK * FOLD, 128), F32),
            dma,
            dma((3,)),
            dma((3,)),
            dma((15,)),
            dma((SEQ,)),
            dma((15,)),
            dma((SEQ,)),
            dma((4,)),
            dma((4,)),
            dma((4, 3)),
            dma((4, 3)),
        ],
        compiler_params=pltpu.CompilerParams(
            collective_id=0, has_side_effects=True, vmem_limit_bytes=50 * 2**20
        ),
        name="attend",
    )(q, k, v, residual, gain, w_out, w_gate, w_up, w_down)


def expert_kernel(
    tok_ref,
    pos_ref,
    gain_ref,
    normed_ref,
    summed_ref,
    res_ref,
    wg_ref,
    wu_ref,
    wd_ref,
    sg_ref,
    su_ref,
    sd_ref,
    out_ref,
    probe_ref,
    send,
    recv,
    back,
    rows_in,
    hidden,
    stage,
    wgu,
    wdn,
    total,
    send_sem,
    recv_sem,
    bsend_sem,
    brecv_sem,
    gu_sem,
    dn_sem,
):
    seq = lax.axis_index("seq")
    ex = lax.axis_index("exp")
    z, x = lax.div(seq, 4), lax.rem(seq, 4)
    y, core = lax.div(ex, 2), lax.rem(ex, 2)

    def peer(i, sign):
        iz = lax.div(i, 16)
        dz = lax.rem(iz, 2) * 2 + lax.div(iz, 2)
        dx = lax.rem(lax.div(i, 4), 4)
        dy = lax.rem(i, 4)
        if sign < 0:
            dz, dx, dy = 4 - dz, 4 - dx, 4 - dy
        return (lax.rem(z + dz, 4) * 4 + lax.rem(x + dx, 4), lax.rem(y + dy, 4) * 2 + core)

    def out_copy(i):
        return pltpu.make_async_remote_copy(
            src_ref=send.at[i],
            dst_ref=recv.at[i],
            send_sem=send_sem.at[i],
            recv_sem=recv_sem.at[i],
            device_id=peer(i, 1),
            device_id_type=MESH,
        )

    def back_copy(i):
        return pltpu.make_async_remote_copy(
            src_ref=recv.at[i],
            dst_ref=back.at[i],
            send_sem=bsend_sem.at[i],
            recv_sem=brecv_sem.at[i],
            device_id=peer(i, -1),
            device_id_type=MESH,
        )

    def gu_start(t, slot):
        lanes = pl.ds(pl.multiple_of(lax.rem(t, 3) * FT, FT), FT)

        def go(gate, up):
            pltpu.make_async_copy(gate.at[0, :, lanes], wgu.at[slot, 0], gu_sem.at[slot, 0]).start()
            pltpu.make_async_copy(up.at[0, :, lanes], wgu.at[slot, 1], gu_sem.at[slot, 1]).start()

        @pl.when(t < 3)
        def _():
            go(wg_ref, wu_ref)

        @pl.when(t >= 3)
        def _():
            go(sg_ref, su_ref)

    def gu_wait(slot):
        pltpu.make_async_copy(wg_ref.at[0, :, :FT], wgu.at[slot, 0], gu_sem.at[slot, 0]).wait()
        pltpu.make_async_copy(wu_ref.at[0, :, :FT], wgu.at[slot, 1], gu_sem.at[slot, 1]).wait()

    def dn_start(n, slot):
        lanes = pl.ds(pl.multiple_of(n * NT, NT), NT)
        pltpu.make_async_copy(wd_ref.at[0, :, lanes], wdn.at[slot, 0], dn_sem.at[slot, 0]).start()
        pltpu.make_async_copy(sd_ref.at[0, :, lanes], wdn.at[slot, 1], dn_sem.at[slot, 1]).start()

    def dn_wait(slot):
        pltpu.make_async_copy(wd_ref.at[0, :, :NT], wdn.at[slot, 0], dn_sem.at[slot, 0]).wait()
        pltpu.make_async_copy(sd_ref.at[0, :, :NT], wdn.at[slot, 1], dn_sem.at[slot, 1]).wait()

    barrier = pltpu.get_barrier_semaphore()

    def greet(i, carry):
        pl.semaphore_signal(barrier, inc=1, device_id=peer(i, 1), device_id_type=MESH)
        return carry

    lax.fori_loop(1, CHIPS, greet, 0)
    gu_start(0, 0)

    for slot in range(SLOTS):
        token = tok_ref[slot]
        for s in range(3):
            recv[0, s * SLOTS + slot] = normed_ref[token, s]
    pl.semaphore_wait(barrier, CHIPS - 1)

    def dispatch(i, carry):
        for slot in range(SLOTS):
            token = tok_ref[i * SLOTS + slot]
            for s in range(3):
                send[i, s * SLOTS + slot] = normed_ref[token, s]
        out_copy(i).start()
        return carry

    lax.fori_loop(1, CHIPS, dispatch, 0)

    def chunk(g, carry):
        def arrive(i, carry):
            out_copy(i).wait_recv()
            return carry

        lax.fori_loop(jnp.where(g == 0, 1, HALF), (g + 1) * HALF, arrive, 0)

        def unfold(m, carry):
            v, part = lax.div(m, 2), lax.rem(m, 2)
            tiles = recv[pl.ds(g * HALF + part * 16, 16), v].astype(F32).reshape(16 * FOLD, LANES)
            for half in (0, 1):
                stage[half, : 16 * FOLD] = tiles[:, half * 128 : half * 128 + 128]
            row = pl.multiple_of(v * HALF + part * 16, 16)
            for c in range(FOLD):
                for half in (0, 1):
                    first = c * LANES + half * 128
                    rows_in[pl.ds(row, 16), first : first + 128] = stage[
                        half, pl.ds(c, 16, stride=FOLD), :
                    ].astype(BF)
            return carry

        lax.fori_loop(0, 2 * VECS, unfold, 0)

        def gate_up(t, carry):
            slot = lax.rem(t, 2)

            @pl.when(t < 5)
            def _():
                gu_start(t + 1, 1 - slot)

            @pl.when(t == 5)
            def _():
                dn_start(0, 0)

            gu_wait(slot)
            g_all = dot(rows_in[...], wgu[slot, 0])
            u_all = dot(rows_in[...], wgu[slot, 1])
            n = SLOTS * HALF
            g0, u0 = g_all[:n], u_all[:n]
            sigma = 1.0 / (1.0 + jnp.exp(-g0))
            active = g0 * sigma
            slope = sigma * (1.0 + g0 * (1.0 - sigma)) * u0
            lanes = pl.ds(pl.multiple_of(t * FT, FT), FT)
            hidden[:n, lanes] = (active * u0).astype(BF)
            hidden[n : 2 * n, lanes] = (slope * g_all[n : 2 * n] + active * u_all[n : 2 * n]).astype(BF)
            hidden[2 * n :, lanes] = (slope * g_all[2 * n :] + active * u_all[2 * n :]).astype(BF)
            return carry

        lax.fori_loop(0, 6, gate_up, 0)

        def down(n, carry):
            slot = lax.rem(n, 2)

            @pl.when(n < 7)
            def _():
                dn_start(n + 1, 1 - slot)

            @pl.when((n == 7) & (g == 0))
            def _():
                gu_start(0, 0)

            dn_wait(slot)
            part = dot(hidden[:, :FH], wdn[slot, 0]) + dot(hidden[:, FH:], wdn[slot, 1])
            for q in range(NT // LANES):
                for half in (0, 1):
                    first = q * LANES + half * 128
                    stage[half, pl.ds(n * (NT // LANES) + q, ROWS, stride=FOLD), :] = part[
                        :, first : first + 128
                    ]
            return carry

        lax.fori_loop(0, D // NT, down, 0)

        def fold(v, carry):
            for part in (0, 1):
                row = pl.multiple_of((v * HALF + part * 16) * FOLD, 256)
                for half in (0, 1):
                    recv[pl.ds(g * HALF + part * 16, 16), v, :, half * 128 : half * 128 + 128] = (
                        stage[half, pl.ds(row, 16 * FOLD), :].reshape(16, FOLD, 128).astype(BF)
                    )
            return carry

        lax.fori_loop(0, VECS, fold, 0)

        def give_back(i, carry):
            back_copy(i).start()
            return carry

        lax.fori_loop(jnp.where(g == 0, 1, HALF), (g + 1) * HALF, give_back, 0)
        return carry

    lax.fori_loop(0, 2, chunk, 0)
    back[0] = recv[0]

    def collect(i, carry):
        out_copy(i).wait_send()
        back_copy(i).wait()
        return carry

    lax.fori_loop(1, CHIPS, collect, 0)

    def combine(tok, carry):
        sums = [jnp.zeros((FOLD, LANES), F32) for _ in range(3)]
        for r in range(8):
            where = pos_ref[tok * 8 + r]
            chip, slot = lax.div(where, SLOTS), lax.rem(where, SLOTS)
            weight = gain_ref[tok * 8 + r]
            for s in range(3):
                sums[s] += weight * back[chip, s * SLOTS + slot].astype(F32)
        row = pl.ds(pl.multiple_of(tok * FOLD, FOLD), FOLD)
        for s in range(3):
            for half in (0, 1):
                total[s, half, row, :] = sums[s][:, half * 128 : half * 128 + 128]
        return carry

    lax.fori_loop(0, TOK, combine, 0)
    probes = [jnp.zeros((TOK, 128), F32) for _ in range(2)]
    for c in range(FOLD):
        for half in (0, 1):
            first = c * LANES + half * 128
            lanes = slice(first, first + 128)
            for s in range(3):
                value = summed_ref[s, :, lanes] + total[s, half, pl.ds(c, TOK, stride=FOLD), :]
                out_ref[s, :, lanes] = value.astype(BF)
                if s:
                    probes[s - 1] += value * res_ref[s, :, lanes].astype(F32)
    for t in range(2):
        mean = jnp.sum(probes[t], axis=1, keepdims=True) * (1.0 / D)
        probe_ref[t] = jnp.broadcast_to(mean, (TOK, 128))


def experts(tok, pos, gains, normed, summed, residual, wg, wu, wd, sg, su, sd):
    smem = pl.BlockSpec(memory_space=pltpu.SMEM)
    vmem = pl.BlockSpec(memory_space=pltpu.VMEM)
    anywhere = pl.BlockSpec(memory_space=pl.ANY)
    dma = pltpu.SemaphoreType.DMA
    tiles = (CHIPS, VECS, FOLD, LANES)
    return pl.pallas_call(
        expert_kernel,
        out_shape=(
            jax.ShapeDtypeStruct((3, TOK, D), BF),
            jax.ShapeDtypeStruct((2, TOK, 128), F32),
        ),
        in_specs=[smem] * 3 + [vmem] * 3 + [anywhere] * 6,
        out_specs=(vmem, vmem),
        scratch_shapes=[
            pltpu.VMEM(tiles, BF),
            pltpu.VMEM(tiles, BF),
            pltpu.VMEM(tiles, BF),
            pltpu.VMEM((ROWS, D), BF),
            pltpu.VMEM((ROWS, 2 * FH), BF),
            pltpu.VMEM((2, ROWS * FOLD, 128), F32),
            pltpu.VMEM((2, 2, D, FT), BF),
            pltpu.VMEM((2, 2, FH, NT), BF),
            pltpu.VMEM((3, 2, TOK * FOLD, 128), F32),
            dma((CHIPS,)),
            dma((CHIPS,)),
            dma((CHIPS,)),
            dma((CHIPS,)),
            dma((2, 2)),
            dma((2, 2)),
        ],
        compiler_params=pltpu.CompilerParams(
            collective_id=1, has_side_effects=True, vmem_limit_bytes=56 * 2**20
        ),
        name="experts",
    )(tok, pos, gains, normed, summed, residual, wg, wu, wd, sg, su, sd)


def plan(routes):
    seq, ex = lax.axis_index("seq"), lax.axis_index("exp")
    z, x, y = seq // 4, seq % 4, ex // 2
    flat = routes.reshape(-1)
    count = flat.shape[0]
    order = jnp.arange(count)
    earlier = (flat[:, None] == flat[None, :]) & (order[None, :] < order[:, None])
    slot = jnp.sum(earlier.astype(jnp.int32), axis=1)
    dz = (flat // 16 - z) % 4
    dx = (flat // 4 % 4 - x) % 4
    dy = (flat % 4 - y) % 4
    number = (dz % 2 * 2 + dz // 2) * 16 + dx * 4 + dy
    pos = number * SLOTS + slot
    hit = (jnp.arange(CHIPS * SLOTS)[:, None] == pos[None, :]).astype(jnp.int32)
    tok = TOK + jnp.sum(hit * (order // 8 - TOK)[None, :], axis=1)
    return tok.astype(jnp.int32), pos.astype(jnp.int32)


def shards(
    queries,
    key_rows,
    value_rows,
    residual,
    w_out,
    norm_gain,
    w_gate,
    w_up,
    w_down,
    routes,
    route_gain,
):
    tok, pos = plan(routes)
    summed, normed, sg, su, sd = attend(
        queries, key_rows, value_rows, residual, norm_gain[None, :], w_out, w_gate, w_up, w_down
    )
    layer_out, probes = experts(
        tok, pos, route_gain.reshape(-1), normed, summed, residual, w_gate, w_up, w_down, sg, su, sd
    )
    return layer_out, probes[:, :, 0]


def solution(mesh):
    return jax.shard_map(
        shards,
        mesh=mesh,
        in_specs=(
            P(None, "seq", "exp"),
            P(None, "seq", "exp"),
            P(None, "seq", "exp"),
            P(None, ("seq", "exp"), None),
            P("exp", None),
            P(),
            P(("seq", "exp"), None, None),
            P(("seq", "exp"), None, None),
            P(("seq", "exp"), None, None),
            P(("seq", "exp"), None),
            P(("seq", "exp"), None),
        ),
        out_specs=(P(None, ("seq", "exp"), None), P(None, ("seq", "exp"))),
        check_vma=False,
    )
```

time: 678 us -> 232 us (0.34)
  the two profiles are of different devices: /device:TPU:2 before, /device:TPU:42 now
where the time goes in v1:
time: 232 us; the launch traced here: 231 us
  Pallas kernels  218 us (94%)
  local copies, waits for them, and re-layouts  11.5 us (5%)
    pallas_call x1, Pallas kernels, experts(): pl.pallas_call(expert_kernel, out_shape=(jax.ShapeDtypeStruct((3, TOK, D)...  163 us
    pallas_call x1, Pallas kernels, attend(): pl.pallas_call(attend_kernel, out_shape=(jax.ShapeDtypeStruct((3, TOK, D)...  55.2 us
    unnamed x19, local copies, waits for them, and re-layouts  9.47 us

profile of v1, /device:TPU:42, one launch (start us, length us, event | category | flops | bytes accessed | tf_op | source)
XLA Modules:
  0.0 231.1 jit_solution(2890323989416545852)
XLA Ops:
  0.7 0.8 copy.17
  1.4 0.1 reshape.167
  1.5 0.2 convert_reduce_fusion
  1.7 0.0 copy-start.7
  1.7 0.1 select_reduce_fusion
  1.9 0.6 broadcast_add_fusion.tok_ref
  2.4 0.8 copy.18
  3.2 0.6 reshape.168.gain_ref
  3.8 0.0 copy-start
  3.8 1.0 copy-done
  4.8 0.0 copy-start.3
  4.8 1.0 copy-done.3
  5.8 0.0 copy-start.4
  5.8 0.9 copy-done.4
  6.7 0.9 copy-done.5
  7.6 0.7 copy-done.6
  8.3 55.2 %attend.1 = (f32[3,16,4096]{2,1,0:T(8,128)S(1)}, bf16[17,3,16,256]{3,2,1,0:T(8,128)(2,1)S(1)}, bf16[1,4096,768]{2,1,0:T(8,128)(2,1)}, bf16[1,4096,768]{2,1,0:T(8,128)(2,1)}, bf16[1,768,4096]{2,1,0:T(8,128)(2,1)}) custom-call(bf16[3,128,512]{2,1,0:T(8,128)(2,1)S(1)} %copy-done.3, bf16[3,128,128]{2,1,0:T(8,128)(2,1)S(1)} %copy-done.4, ...), custom_call_target="tpu_custom_call" | custom-call | tf_op jit(solution)/shard_map/attend/pallas_call | solution.py:279
  63.5 0.0 copy-done.7
  63.5 0.0 copy-start.1
  63.5 0.9 copy-done.1
  64.4 0.8 copy-done.2
  65.2 162.8 %experts.1 = (bf16[3,16,4096]{2,1,0:T(8,128)(2,1)}, f32[2,16,128]{2,1,0:T(8,128)}) custom-call(s32[192]{0:T(256)} %broadcast_add_fusion.tok_ref, s32[128]{0:T(128)} %copy-done.7, f32[128]{0:T(128)} %reshape.168.gain_ref, bf16[17,3,16,256]{3,2,1,0:T(8,128)(2,1)} %copy-done.2, f32[3,16,4096]{2,1,0:T(8,128)} %copy-done.1, bf16[3,16,4096]{2,1,0:T(8,128)(2,1)} %res_ref.3, ...), custom_call_target="tpu_custom_call" | custom-call | tf_op jit(solution)/shard_map/experts/pallas_call | solution.py:579
  228.0 1.4 slice_reduce_fusion
  229.4 1.8 copy.20
  (4 shorter events, 0.0 us)
Async XLA Ops:
  1.7 61.7 %copy-start.7 = (s32[128]{0:T(128)}, s32[128]{0:T(128)S(1)}, u32[]{:S(2)}) copy-start(s32[128]{0:T(128)S(1)} %get-tuple-element.17.pos_ref) | copy-start | bytes 1540
  3.8 1.0 copy-start
  4.8 1.0 copy-start.3
  5.8 0.9 copy-start.4
  6.7 0.9 copy-start.5
  7.6 0.7 copy-start.6
  63.5 0.9 copy-start.1
  64.4 0.8 copy-start.2

commit v2 on v0

v2 whole, which is shorter than its diff:
```python
import math

import jax
import jax.numpy as jnp
from jax import lax
from jax.experimental import pallas as pl
from jax.experimental.pallas import tpu as pltpu
from jax.sharding import PartitionSpec as P

HD = 128
EPS = 1e-06
MESH = pl.DeviceIdType.MESH
BF = jnp.bfloat16
F32 = jnp.float32

SEQ = 16
KEYS = 128
TOK = 16
D = 4096
LANES = 256
FOLD = D // LANES
CHIPS = 64
SLOTS = 3
VECS = 3 * SLOTS
FH = 768
HALF = 32
ROWS = HALF * VECS
FT = 256
WINDOW = 24
NT = 512


def dot(a, b):
    return jnp.dot(a, b, preferred_element_type=F32)


def dot_nt(a, b):
    return lax.dot_general(a, b, (((1,), (1,)), ((), ())), preferred_element_type=F32)


def layer_kernel(
    tok_ref,
    pos_ref,
    gains_ref,
    q_hbm,
    k_hbm,
    v_hbm,
    res_hbm,
    gain_hbm,
    wo_hbm,
    wg_ref,
    wu_ref,
    wd_ref,
    out_ref,
    probe_ref,
    sg_ref,
    su_ref,
    sd_ref,
    q_ref,
    res_ref,
    gain_ref,
    summed_ref,
    normed_ref,
    kb,
    vb,
    sib_send,
    sib_recv,
    own,
    y_send,
    y_recv,
    send,
    recv,
    back,
    total,
    in_sem,
    w_send,
    w_recv,
    k_send,
    k_recv,
    v_send,
    v_recv,
    s_send,
    s_recv,
    ys_send,
    ys_recv,
    send_sem,
    recv_sem,
    bsend_sem,
    brecv_sem,
    gu_sem,
    dn_sem,
):
    seq = lax.axis_index("seq")
    ex = lax.axis_index("exp")
    z, x = lax.div(seq, 4), lax.rem(seq, 4)
    y, core = lax.div(ex, 2), lax.rem(ex, 2)
    sibling = (seq, y * 2 + (1 - core))
    scale = 1.0 / math.sqrt(HD)
    order = (1, 3, 2)

    def z_peer(d):
        return (lax.rem(z + d, 4) * 4 + x, ex)

    def x_peer(d):
        return (z * 4 + lax.rem(x + d, 4), ex)

    def y_peer(d):
        return (seq, lax.rem(y + d, 4) * 2 + core)

    def peer(i, sign):
        iz = lax.div(i, 16)
        dz = lax.rem(iz, 2) * 2 + lax.div(iz, 2)
        dx = lax.rem(lax.div(i, 4), 4)
        dy = lax.rem(i, 4)
        if sign < 0:
            dz, dx, dy = 4 - dz, 4 - dx, 4 - dy
        return (lax.rem(z + dz, 4) * 4 + lax.rem(x + dx, 4), lax.rem(y + dy, 4) * 2 + core)

    def remote(src, dst, ssem, rsem, peer):
        return pltpu.make_async_remote_copy(
            src_ref=src, dst_ref=dst, send_sem=ssem, recv_sem=rsem, device_id=peer, device_id_type=MESH
        )

    barrier = pltpu.get_barrier_semaphore()
    pl.semaphore_signal(barrier, inc=1, device_id=sibling, device_id_type=MESH)

    def greet(i, carry):
        pl.semaphore_signal(barrier, inc=1, device_id=peer(i, 1), device_id_type=MESH)
        return carry

    lax.fori_loop(1, CHIPS, greet, 0)
    k_in = pltpu.make_async_copy(k_hbm, kb.at[seq], in_sem.at[0])
    v_in = pltpu.make_async_copy(v_hbm, vb.at[seq], in_sem.at[1])
    q_in = pltpu.make_async_copy(q_hbm, q_ref, in_sem.at[2])
    res_in = pltpu.make_async_copy(res_hbm, res_ref, in_sem.at[3])
    gain_in = pltpu.make_async_copy(gain_hbm, gain_ref, in_sem.at[4])
    for copy in (k_in, v_in, q_in, res_in, gain_in):
        copy.start()
    k_in.wait()
    v_in.wait()
    pl.semaphore_wait(barrier, CHIPS)

    weight_copies = [
        remote(wg_ref, sg_ref, w_send.at[0], w_recv.at[0], sibling),
        remote(wu_ref, su_ref, w_send.at[1], w_recv.at[1], sibling),
        remote(wd_ref, sd_ref, w_send.at[2], w_recv.at[2], sibling),
    ]

    def k_copy(origin, number, peer):
        return remote(kb.at[origin], kb.at[origin], k_send.at[number], k_recv.at[origin], peer)

    def v_copy(origin, number, peer):
        return remote(vb.at[origin], vb.at[origin], v_send.at[number], v_recv.at[origin], peer)

    for d in order:
        k_copy(seq, d - 1, z_peer(d)).start()
        v_copy(seq, d - 1, x_peer(d)).start()
    for d in order:
        k_copy(seq, 3 + d - 1, x_peer(d)).start()
        v_copy(seq, 3 + d - 1, z_peer(d)).start()
    for copy in weight_copies:
        copy.start()

    def attend(qs, qc, scores, slopes, att, wo):
        wo_copy = pltpu.make_async_copy(wo_hbm, wo, in_sem.at[5])
        wo_copy.start()
        q_in.wait()
        for h in range(4):
            for s in range(3):
                qs[s, h * 128 : (h + 1) * 128, :] = q_ref[s, :, h * 128 : (h + 1) * 128]
        for t in (1, 2):
            qc[t - 1, :, :HD] = qs[t]
            qc[t - 1, :, HD:] = qs[0]

        for d in order:
            from_z = lax.rem(z + d, 4) * 4 + x
            from_x = z * 4 + lax.rem(x + d, 4)
            k_copy(from_z, 0, z_peer(d)).wait_recv()
            for e in order:
                k_copy(from_z, 3 * (d + 1) + e - 1, x_peer(e)).start()
            v_copy(from_x, 0, x_peer(d)).wait_recv()
            for e in order:
                v_copy(from_x, 3 * (d + 1) + e - 1, z_peer(e)).start()

        for dz in (0,) + order:
            c = lax.rem(z + dz, 4)
            for e in (1, 2, 3):
                k_copy(c * 4 + lax.rem(x + e, 4), 0, x_peer(e)).wait_recv()
            kc = kb[pl.ds(c * 4, 4)]
            k0 = kc[:, 0].reshape(512, HD)
            scores[c] = dot_nt(qs[0], k0) * scale
            for t in (1, 2):
                kt = kc[:, t].reshape(512, HD)
                slopes[t - 1, c] = dot_nt(qc[t - 1], jnp.concatenate([k0, kt], axis=1)) * scale

        for d in order:
            for e in (0, 1, 2, 3):
                origin = lax.rem(z + d, 4) * 4 + lax.rem(x + e, 4)
                v_copy(origin, 0, z_peer(d)).wait_recv()

        def head(h, carry):
            rows = pl.ds(pl.multiple_of(h * 128, 128), 128)
            top = jnp.max(scores[0, rows, :], axis=1, keepdims=True)
            for c in (1, 2, 3):
                top = jnp.maximum(top, jnp.max(scores[c, rows, :], axis=1, keepdims=True))
            norm = jnp.zeros((128, 1), F32)
            r1 = jnp.zeros((128, 1), F32)
            r2 = jnp.zeros((128, 1), F32)
            acc = jnp.zeros((128, 3 * HD), F32)
            mixed = jnp.zeros((256, HD), F32)
            for c in range(4):
                p = jnp.exp(scores[c, rows, :] - top).astype(BF)
                pf = p.astype(F32)
                w1 = (pf * slopes[0, c, rows, :]).astype(BF)
                w2 = (pf * slopes[1, c, rows, :]).astype(BF)
                norm += jnp.sum(pf, axis=1, keepdims=True)
                r1 += jnp.sum(w1.astype(F32), axis=1, keepdims=True)
                r2 += jnp.sum(w2.astype(F32), axis=1, keepdims=True)
                v0 = vb[4 * c : 4 * c + 4, 0].reshape(512, HD)
                v1 = vb[4 * c : 4 * c + 4, 1].reshape(512, HD)
                v2 = vb[4 * c : 4 * c + 4, 2].reshape(512, HD)
                acc += dot(p, jnp.concatenate([v0, v1, v2], axis=1))
                mixed += dot(jnp.concatenate([w1, w2], axis=0), v0)
            inv = 1.0 / norm
            main = acc[:, :HD] * inv
            t1 = (mixed[:128] + acc[:, HD : 2 * HD]) * inv - (r1 * inv) * main
            t2 = (mixed[128:] + acc[:, 2 * HD :]) * inv - (r2 * inv) * main
            att[0, :, rows] = main.astype(BF)
            att[1, :, rows] = t1.astype(BF)
            att[2, :, rows] = t2.astype(BF)
            return carry

        lax.fori_loop(0, 4, head, 0)

        wo_copy.wait()

        def block_rows(parity):
            parts = []
            for d in range(4):
                j = lax.rem(y + d, 4) * 2 + parity
                rows = pl.ds(pl.multiple_of(j * TOK, TOK), TOK)
                for s in range(3):
                    parts.append(att[s, rows, :])
            return jnp.concatenate(parts, axis=0)

        sib_rows = block_rows(1 - core)
        sib_copies = []
        for n in range(4):
            sib_send[n] = dot(sib_rows, wo[:, n * 1024 : (n + 1) * 1024]).astype(BF)
            copy = remote(sib_send.at[n], sib_recv.at[n], s_send.at[n], s_recv.at[n], sibling)
            copy.start()
            sib_copies.append(copy)
        own_rows = block_rows(core)
        y_copies = []
        for n in range(4):
            lanes = slice(n * 1024, (n + 1) * 1024)
            product = dot(own_rows, wo[:, lanes])
            sib_copies[n].wait_recv()
            both = product + sib_recv[n].astype(F32)
            own[:, lanes] = both[:48]
            for d in order:
                y_send[n, d - 1] = both[48 * d : 48 * (d + 1)].astype(BF)
                copy = remote(
                    y_send.at[n, d - 1], y_recv.at[n, d - 1], ys_send.at[n, d - 1], ys_recv.at[n, d - 1], y_peer(d)
                )
                copy.start()
                y_copies.append(copy)
        res_in.wait()
        for n in range(4):
            for d in (1, 2, 3):
                y_copies[n * 3 + order.index(d)].wait_recv()
            lanes = slice(n * 1024, (n + 1) * 1024)
            part = own[:, lanes]
            for d in (1, 2, 3):
                part += y_recv[n, d - 1].astype(F32)
            for s in range(3):
                summed_ref[s, :, lanes] = part[16 * s : 16 * (s + 1)] + res_ref[s, :, lanes].astype(F32)
        for d in order:
            k_copy(seq, d - 1, z_peer(d)).wait_send()
            v_copy(seq, d - 1, x_peer(d)).wait_send()
        for number in range(3, 15):
            k_copy(seq, number, x_peer(1)).wait_send()
            v_copy(seq, number, z_peer(1)).wait_send()
        for copy in sib_copies + y_copies:
            copy.wait_send()

    pl.run_scoped(
        attend,
        pltpu.VMEM((3, 512, HD), BF),
        pltpu.VMEM((2, 512, 2 * HD), BF),
        pltpu.VMEM((4, 512, 512), F32),
        pltpu.VMEM((2, 4, 512, 512), F32),
        pltpu.VMEM((3, KEYS, 512), BF),
        pltpu.VMEM((512, D), BF),
    )

    def out_copy(i):
        return remote(send.at[i], recv.at[i], send_sem.at[i], recv_sem.at[i], peer(i, 1))

    def back_copy(i):
        return remote(recv.at[i], back.at[i], bsend_sem.at[i], brecv_sem.at[i], peer(i, -1))

    def moe(rows_in, hidden, stage, wgu, wdn):
        def gu_start(t, slot):
            lanes = pl.ds(pl.multiple_of(lax.rem(t, 3) * FT, FT), FT)

            def go(gate, up):
                pltpu.make_async_copy(gate.at[0, :, lanes], wgu.at[slot, 0], gu_sem.at[slot, 0]).start()
                pltpu.make_async_copy(up.at[0, :, lanes], wgu.at[slot, 1], gu_sem.at[slot, 1]).start()

            @pl.when(t < 3)
            def _():
                go(wg_ref, wu_ref)

            @pl.when(t >= 3)
            def _():
                go(sg_ref, su_ref)

        def gu_wait(slot):
            pltpu.make_async_copy(wg_ref.at[0, :, :FT], wgu.at[slot, 0], gu_sem.at[slot, 0]).wait()
            pltpu.make_async_copy(wu_ref.at[0, :, :FT], wgu.at[slot, 1], gu_sem.at[slot, 1]).wait()

        def dn_start(n, slot):
            lanes = pl.ds(pl.multiple_of(n * NT, NT), NT)
            pltpu.make_async_copy(wd_ref.at[0, :, lanes], wdn.at[slot, 0], dn_sem.at[slot, 0]).start()
            pltpu.make_async_copy(sd_ref.at[0, :, lanes], wdn.at[slot, 1], dn_sem.at[slot, 1]).start()

        def dn_wait(slot):
            pltpu.make_async_copy(wd_ref.at[0, :, :NT], wdn.at[slot, 0], dn_sem.at[slot, 0]).wait()
            pltpu.make_async_copy(sd_ref.at[0, :, :NT], wdn.at[slot, 1], dn_sem.at[slot, 1]).wait()

        gu_start(0, 0)

        gain_in.wait()
        main_sum = summed_ref[0]
        recip = lax.rsqrt(jnp.mean(main_sum * main_sum, axis=-1, keepdims=True) + EPS)
        normed_ref[TOK] = jnp.zeros((3, FOLD, LANES), BF)
        for s in range(3):
            if s == 0:
                rows = main_sum * recip * gain_ref[...]
            else:
                inner = jnp.mean(main_sum * summed_ref[s], axis=-1, keepdims=True)
                rows = (summed_ref[s] * recip - main_sum * (recip * recip * recip * inner)) * gain_ref[...]
            for c in range(FOLD):
                for half in (0, 1):
                    first = c * LANES + half * 128
                    stage[half, pl.ds(c, TOK, stride=FOLD), :] = rows[:, first : first + 128]
            for half in (0, 1):
                normed_ref[:TOK, s, :, half * 128 : half * 128 + 128] = (
                    stage[half, : TOK * FOLD].reshape(TOK, FOLD, 128).astype(BF)
                )

        def dispatch(i, carry):
            for slot in range(SLOTS):
                token = tok_ref[i * SLOTS + slot]
                for s in range(3):
                    send[i, s * SLOTS + slot] = normed_ref[token, s]

            @pl.when(i > WINDOW)
            def _():
                out_copy(i - WINDOW).wait_send()

            out_copy(i).start()
            return carry

        lax.fori_loop(1, CHIPS, dispatch, 0)

        for slot in range(SLOTS):
            token = tok_ref[slot]
            for s in range(3):
                recv[0, s * SLOTS + slot] = normed_ref[token, s]
        for copy in weight_copies:
            copy.wait()

        def chunk(g, carry):
            def arrive(i, carry):
                out_copy(i).wait_recv()
                return carry

            lax.fori_loop(jnp.where(g == 0, 1, HALF), (g + 1) * HALF, arrive, 0)

            def unfold(m, carry):
                v, part = lax.div(m, 2), lax.rem(m, 2)
                tiles = recv[pl.ds(g * HALF + part * 16, 16), v].astype(F32).reshape(16 * FOLD, LANES)
                for half in (0, 1):
                    stage[half, : 16 * FOLD] = tiles[:, half * 128 : half * 128 + 128]
                row = pl.multiple_of(v * HALF + part * 16, 16)
                for c in range(FOLD):
                    for half in (0, 1):
                        first = c * LANES + half * 128
                        rows_in[pl.ds(row, 16), first : first + 128] = stage[
                            half, pl.ds(c, 16, stride=FOLD), :
                        ].astype(BF)
                return carry

            lax.fori_loop(0, 2 * VECS, unfold, 0)

            def gate_up(t, carry):
                slot = lax.rem(t, 2)

                @pl.when(t < 5)
                def _():
                    gu_start(t + 1, 1 - slot)

                @pl.when(t == 5)
                def _():
                    dn_start(0, 0)

                gu_wait(slot)
                g_all = dot(rows_in[...], wgu[slot, 0])
                u_all = dot(rows_in[...], wgu[slot, 1])
                n = SLOTS * HALF
                g0, u0 = g_all[:n], u_all[:n]
                sigma = 1.0 / (1.0 + jnp.exp(-g0))
                active = g0 * sigma
                slope = sigma * (1.0 + g0 * (1.0 - sigma)) * u0
                lanes = pl.ds(pl.multiple_of(t * FT, FT), FT)
                hidden[:n, lanes] = (active * u0).astype(BF)
                hidden[n : 2 * n, lanes] = (slope * g_all[n : 2 * n] + active * u_all[n : 2 * n]).astype(BF)
                hidden[2 * n :, lanes] = (slope * g_all[2 * n :] + active * u_all[2 * n :]).astype(BF)
                return carry

            lax.fori_loop(0, 6, gate_up, 0)

            def down(n, carry):
                slot = lax.rem(n, 2)

                @pl.when(n < D // NT - 1)
                def _():
                    dn_start(n + 1, 1 - slot)

                @pl.when((n == D // NT - 1) & (g == 0))
                def _():
                    gu_start(0, 0)

                dn_wait(slot)
                part = dot(hidden[:, :FH], wdn[slot, 0]) + dot(hidden[:, FH:], wdn[slot, 1])
                for q in range(NT // LANES):
                    for half in (0, 1):
                        first = q * LANES + half * 128
                        stage[half, pl.ds(n * (NT // LANES) + q, ROWS, stride=FOLD), :] = part[
                            :, first : first + 128
                        ]
                return carry

            lax.fori_loop(0, D // NT, down, 0)

            def fold(v, carry):
                for part in (0, 1):
                    row = pl.multiple_of((v * HALF + part * 16) * FOLD, 256)
                    for half in (0, 1):
                        recv[pl.ds(g * HALF + part * 16, 16), v, :, half * 128 : half * 128 + 128] = (
                            stage[half, pl.ds(row, 16 * FOLD), :].reshape(16, FOLD, 128).astype(BF)
                        )
                return carry

            lax.fori_loop(0, VECS, fold, 0)

            def give_back(i, carry):
                back_copy(i).start()
                return carry

            lax.fori_loop(jnp.where(g == 0, 1, HALF), (g + 1) * HALF, give_back, 0)
            return carry

        lax.fori_loop(0, 2, chunk, 0)

    pl.run_scoped(
        moe,
        pltpu.VMEM((ROWS, D), BF),
        pltpu.VMEM((ROWS, 2 * FH), BF),
        pltpu.VMEM((2, ROWS * FOLD, 128), F32),
        pltpu.VMEM((2, 2, D, FT), BF),
        pltpu.VMEM((2, 2, FH, NT), BF),
    )
    back[0] = recv[0]

    def collect(i, carry):
        @pl.when(i >= CHIPS - WINDOW)
        def _():
            out_copy(i).wait_send()

        back_copy(i).wait()
        return carry

    lax.fori_loop(1, CHIPS, collect, 0)

    def combine(tok, carry):
        sums = [jnp.zeros((FOLD, LANES), F32) for _ in range(3)]
        for r in range(8):
            where = pos_ref[r * TOK + tok]
            chip, slot = lax.div(where, SLOTS), lax.rem(where, SLOTS)
            weight = gains_ref[r, tok]
            for s in range(3):
                sums[s] += weight * back[chip, s * SLOTS + slot].astype(F32)
        row = pl.ds(pl.multiple_of(tok * FOLD, FOLD), FOLD)
        for s in range(3):
            for half in (0, 1):
                total[s, half, row, :] = sums[s][:, half * 128 : half * 128 + 128]
        return carry

    lax.fori_loop(0, TOK, combine, 0)
    probes = [jnp.zeros((TOK, 128), F32) for _ in range(2)]
    for c in range(FOLD):
        for half in (0, 1):
            first = c * LANES + half * 128
            lanes = slice(first, first + 128)
            for s in range(3):
                value = summed_ref[s, :, lanes] + total[s, half, pl.ds(c, TOK, stride=FOLD), :]
                out_ref[s, :, lanes] = value.astype(BF)
                if s:
                    probes[s - 1] += value * res_ref[s, :, lanes].astype(F32)
    diagonal = lax.broadcasted_iota(jnp.int32, (TOK, 128), 0) == lax.broadcasted_iota(jnp.int32, (TOK, 128), 1)
    for t in range(2):
        mean = jnp.sum(probes[t], axis=1, keepdims=True) * (1.0 / D)
        flat = jnp.sum(jnp.where(diagonal, mean, 0.0), axis=0, keepdims=True)
        probe_ref[t : t + 1, :] = flat[:, :TOK]


def layer(tok, pos, gains, q, k, v, residual, gain, w_out, w_gate, w_up, w_down):
    smem = pl.BlockSpec(memory_space=pltpu.SMEM)
    vmem = pl.BlockSpec(memory_space=pltpu.VMEM)
    hbm = pl.BlockSpec(memory_space=pltpu.HBM)
    dma = pltpu.SemaphoreType.DMA
    tiles = (CHIPS, VECS, FOLD, LANES)
    outs = pl.pallas_call(
        layer_kernel,
        out_shape=(
            jax.ShapeDtypeStruct((3, TOK, D), BF),
            jax.ShapeDtypeStruct((2, TOK), F32),
            jax.ShapeDtypeStruct(w_gate.shape, BF),
            jax.ShapeDtypeStruct(w_up.shape, BF),
            jax.ShapeDtypeStruct(w_down.shape, BF),
        ),
        in_specs=[smem] * 3 + [hbm] * 9,
        out_specs=(vmem, vmem, hbm, hbm, hbm),
        scratch_shapes=[
            pltpu.VMEM((3, KEYS, 512), BF),
            pltpu.VMEM((3, TOK, D), BF),
            pltpu.VMEM((1, D), F32),
            pltpu.VMEM((3, TOK, D), F32),
            pltpu.VMEM((TOK + 1, 3, FOLD, LANES), BF),
            pltpu.VMEM((SEQ, 3, KEYS, HD), BF),
            pltpu.VMEM((SEQ, 3, KEYS, HD), BF),
            pltpu.VMEM((4, 192, 1024), BF),
            pltpu.VMEM((4, 192, 1024), BF),
            pltpu.VMEM((48, D), F32),
            pltpu.VMEM((4, 3, 48, 1024), BF),
            pltpu.VMEM((4, 3, 48, 1024), BF),
            pltpu.VMEM(tiles, BF),
            pltpu.VMEM(tiles, BF),
            pltpu.VMEM(tiles, BF),
            pltpu.VMEM((3, 2, TOK * FOLD, 128), F32),
            dma((6,)),
            dma((3,)),
            dma((3,)),
            dma((15,)),
            dma((SEQ,)),
            dma((15,)),
            dma((SEQ,)),
            dma((4,)),
            dma((4,)),
            dma((4, 3)),
            dma((4, 3)),
            dma((CHIPS,)),
            dma((CHIPS,)),
            dma((CHIPS,)),
            dma((CHIPS,)),
            dma((2, 2)),
            dma((2, 2)),
        ],
        compiler_params=pltpu.CompilerParams(
            collective_id=0, has_side_effects=True, vmem_limit_bytes=58 * 2**20
        ),
        name="layer",
    )(tok, pos, gains, q, k, v, residual, gain, w_out, w_gate, w_up, w_down)
    return outs[0], outs[1]


def plan(routes):
    seq, ex = lax.axis_index("seq"), lax.axis_index("exp")
    z, x, y = seq // 4, seq % 4, ex // 2
    flat = routes.T.reshape(-1)
    count = flat.shape[0]
    order = jnp.arange(count)
    earlier = (flat[:, None] == flat[None, :]) & (order[None, :] < order[:, None])
    slot = jnp.sum(earlier.astype(jnp.int32), axis=1)
    dz = (flat // 16 - z) % 4
    dx = (flat // 4 % 4 - x) % 4
    dy = (flat % 4 - y) % 4
    number = (dz % 2 * 2 + dz // 2) * 16 + dx * 4 + dy
    pos = number * SLOTS + slot
    hit = (jnp.arange(CHIPS * SLOTS)[:, None] == pos[None, :]).astype(jnp.int32)
    tok = TOK + jnp.sum(hit * (order % TOK - TOK)[None, :], axis=1)
    return tok.astype(jnp.int32), pos.astype(jnp.int32)


def shards(
    queries,
    key_rows,
    value_rows,
    residual,
    w_out,
    norm_gain,
    w_gate,
    w_up,
    w_down,
    routes,
    route_gain,
):
    tok, pos = plan(routes)
    return layer(
        tok,
        pos,
        route_gain.T,
        queries,
        key_rows,
        value_rows,
        residual,
        norm_gain[None, :],
        w_out,
        w_gate,
        w_up,
        w_down,
    )


def solution(mesh):
    return jax.shard_map(
        shards,
        mesh=mesh,
        in_specs=(
            P(None, "seq", "exp"),
            P(None, "seq", "exp"),
            P(None, "seq", "exp"),
            P(None, ("seq", "exp"), None),
            P("exp", None),
            P(),
            P(("seq", "exp"), None, None),
            P(("seq", "exp"), None, None),
            P(("seq", "exp"), None, None),
            P(("seq", "exp"), None),
            P(("seq", "exp"), None),
        ),
        out_specs=(P(None, ("seq", "exp"), None), P(None, ("seq", "exp"))),
        check_vma=False,
    )
```

time: 678 us -> 228 us (0.34)
  waiting for transfers between devices: 275 us -> 0 us
  Pallas kernels: 0 us -> 219 us
  blocking collectives: 150 us -> 0 us
  local copies, waits for them, and re-layouts: 144 us -> 3.77 us
  matrix products: 47.6 us -> 0 us
  other arithmetic: 30.4 us -> 0.9 us
  between operations: 14.4 us -> 0.69 us
    pallas_call x0 -> x1, Pallas kernels: none -> 219 us  [layer(): pl.pallas_call(layer_kernel, out_shape=(jax.ShapeDtypeStruct((3, TOK, D),...]
    all_to_all x1 -> x0, waiting for transfers between devices: 153 us -> none  [shards(): lax.all_to_all(produced, ('seq', 'exp'), split_axis=0, concat_axis=0, til...]
    all_to_all x1 -> x0, blocking collectives: 150 us -> none  [shards(): lax.all_to_all(send_both, ('seq', 'exp'), split_axis=0, concat_axis=0, ti...]
    all_gather x2 -> x0, waiting for transfers between devices: 86.4 us -> none  [the longest x1 45.1 us: shards(): key_piece = lax.all_gather(key_rows, 'seq', axis=1, tiled=True)]
    reshape x5 -> x1, local copies, waits for them, and re-layouts: 63.8 us -> 0.77 us  [plan(): flat = routes.T.reshape(-1)]
    dot_general x12 -> x0, matrix products: 47.6 us -> none  [the longest x1 12 us: shards(): jnp.einsum('rsd,df->rsf', flat_rows, w_up[0], preferred_element_type=jnp....]
    reduce_scatter x1 -> x0, waiting for transfers between devices: 34.7 us -> none  [shards(): lax.psum_scatter(jnp.einsum('sqh,hd->qsd', attended, w_out, preferred_ele...]
    scatter x2 -> x0, local copies, waits for them, and re-layouts: 29.9 us -> none  [shards(): send_once = send_once.at[flat_routes, slot_of].set(normed[token_of])]
  transfers between devices with their start and end apart: 4 -> 0, of which waited for: 4 -> 0; matrix products, arithmetic and copies ran while one was open for 1% -> 0% of each run, Pallas kernels for 0% -> 0%
where the time goes in v2:
time: 228 us; the launch traced here: 224 us
  Pallas kernels  219 us (96%)
  local copies, waits for them, and re-layouts  3.77 us (2%)
    pallas_call x1, Pallas kernels, layer(): pl.pallas_call(layer_kernel, out_shape=(jax.ShapeDtypeStruct((3, TOK, D),...  219 us

profile of v2, /device:TPU:2, one launch (start us, length us, event | category | flops | bytes accessed | tf_op | source)
XLA Modules:
  0.0 224.0 jit_solution(3957922403210436992)
XLA Ops:
  0.7 0.8 reshape.160
  1.4 0.2 convert_reduce_fusion
  1.6 0.0 copy-start
  1.7 0.1 select_reduce_fusion
  1.8 0.6 broadcast_add_fusion.tok_ref
  2.3 0.0 copy-done
  2.3 218.7 %layer.1 = (bf16[3,16,4096]{2,1,0:T(8,128)(2,1)}, f32[2,16]{1,0:T(2,128)}, bf16[1,4096,768]{2,1,0:T(8,128)(2,1)}, bf16[1,4096,768]{2,1,0:T(8,128)(2,1)}, bf16[1,768,4096]{2,1,0:T(8,128)(2,1)}) custom-call(s32[192]{0:T(256)} %broadcast_add_fusion.tok_ref, s32[128]{0:T(128)} %copy-done, f32[8,16]{1,0:T(8,128)} %bitcast.4, bf16[3,128,512]{2,1,0:T(8,128)(2,1)} %q_hbm.1, ...), custom_call_target="tpu_custom_call" | custom-call | tf_op jit(solution)/shard_map/layer/pallas_call | solution.py:526
  221.0 1.8 copy.15
  222.8 1.2 copy.16
  (1 shorter events, 0.0 us)
Async XLA Ops:
  1.6 0.7 copy-start

commit v3 on v2

--- a/solution.py
+++ b/solution.py
@@ -140,11 +140,13 @@
     v_in.wait()
     pl.semaphore_wait(barrier, CHIPS)
 
-    weight_copies = [
-        remote(wg_ref, sg_ref, w_send.at[0], w_recv.at[0], sibling),
-        remote(wu_ref, su_ref, w_send.at[1], w_recv.at[1], sibling),
-        remote(wd_ref, sd_ref, w_send.at[2], w_recv.at[2], sibling),
-    ]
+    def weight_copy(which, part):
+        source = (wg_ref, wu_ref, wd_ref)[which]
+        place = (sg_ref, su_ref, sd_ref)[which]
+        count = (D, D, FH)[which] // 4
+        rows = pl.ds(pl.multiple_of(part * count, count), count)
+        number = which * 4 + part
+        return remote(source.at[0, rows, :], place.at[0, rows, :], w_send.at[number], w_recv.at[number], sibling)
 
     def k_copy(origin, number, peer):
         return remote(kb.at[origin], kb.at[origin], k_send.at[number], k_recv.at[origin], peer)
@@ -158,12 +160,12 @@
     for d in order:
         k_copy(seq, 3 + d - 1, x_peer(d)).start()
         v_copy(seq, 3 + d - 1, z_peer(d)).start()
-    for copy in weight_copies:
-        copy.start()
+    weight_copy(0, 0).start()
+    weight_copy(0, 1).start()
 
     def attend(qs, qc, scores, slopes, att, wo):
         wo_copy = pltpu.make_async_copy(wo_hbm, wo, in_sem.at[5])
-        wo_copy.start()
+        wo_copy.start(priority=1)
         q_in.wait()
         for h in range(4):
             for s in range(3):
@@ -181,11 +183,14 @@
             v_copy(from_x, 0, x_peer(d)).wait_recv()
             for e in order:
                 v_copy(from_x, 3 * (d + 1) + e - 1, z_peer(e)).start()
+            if d != 2:
+                weight_copy(0, 2 + order.index(d)).start()
 
         for dz in (0,) + order:
             c = lax.rem(z + dz, 4)
             for e in (1, 2, 3):
                 k_copy(c * 4 + lax.rem(x + e, 4), 0, x_peer(e)).wait_recv()
+            weight_copy(1, dz).start()
             kc = kb[pl.ds(c * 4, 4)]
             k0 = kc[:, 0].reshape(512, HD)
             scores[c] = dot_nt(qs[0], k0) * scale
@@ -199,6 +204,7 @@
                 v_copy(origin, 0, z_peer(d)).wait_recv()
 
         def head(h, carry):
+            weight_copy(2, h).start()
             rows = pl.ds(pl.multiple_of(h * 128, 128), 128)
             top = jnp.max(scores[0, rows, :], axis=1, keepdims=True)
             for c in (1, 2, 3):
@@ -301,12 +307,20 @@
         return remote(recv.at[i], back.at[i], bsend_sem.at[i], brecv_sem.at[i], peer(i, -1))
 
     def moe(rows_in, hidden, stage, wgu, wdn):
+        def gu_copy(source, which, lanes, slot):
+            place = wgu.at[slot, :, which * FT : (which + 1) * FT]
+            return pltpu.make_async_copy(source.at[0, :, lanes], place, gu_sem.at[slot, which])
+
+        def dn_copy(source, which, lanes, slot):
+            place = wdn.at[slot, which * FH : (which + 1) * FH, :]
+            return pltpu.make_async_copy(source.at[0, :, lanes], place, dn_sem.at[slot, which])
+
         def gu_start(t, slot):
             lanes = pl.ds(pl.multiple_of(lax.rem(t, 3) * FT, FT), FT)
 
             def go(gate, up):
-                pltpu.make_async_copy(gate.at[0, :, lanes], wgu.at[slot, 0], gu_sem.at[slot, 0]).start()
-                pltpu.make_async_copy(up.at[0, :, lanes], wgu.at[slot, 1], gu_sem.at[slot, 1]).start()
+                gu_copy(gate, 0, lanes, slot).start(priority=1)
+                gu_copy(up, 1, lanes, slot).start(priority=1)
 
             @pl.when(t < 3)
             def _():
@@ -317,17 +331,17 @@
                 go(sg_ref, su_ref)
 
         def gu_wait(slot):
-            pltpu.make_async_copy(wg_ref.at[0, :, :FT], wgu.at[slot, 0], gu_sem.at[slot, 0]).wait()
-            pltpu.make_async_copy(wu_ref.at[0, :, :FT], wgu.at[slot, 1], gu_sem.at[slot, 1]).wait()
+            gu_copy(wg_ref, 0, slice(0, FT), slot).wait()
+            gu_copy(wu_ref, 1, slice(0, FT), slot).wait()
 
         def dn_start(n, slot):
             lanes = pl.ds(pl.multiple_of(n * NT, NT), NT)
-            pltpu.make_async_copy(wd_ref.at[0, :, lanes], wdn.at[slot, 0], dn_sem.at[slot, 0]).start()
-            pltpu.make_async_copy(sd_ref.at[0, :, lanes], wdn.at[slot, 1], dn_sem.at[slot, 1]).start()
+            dn_copy(wd_ref, 0, lanes, slot).start(priority=1)
+            dn_copy(sd_ref, 1, lanes, slot).start(priority=1)
 
         def dn_wait(slot):
-            pltpu.make_async_copy(wd_ref.at[0, :, :NT], wdn.at[slot, 0], dn_sem.at[slot, 0]).wait()
-            pltpu.make_async_copy(sd_ref.at[0, :, :NT], wdn.at[slot, 1], dn_sem.at[slot, 1]).wait()
+            dn_copy(wd_ref, 0, slice(0, NT), slot).wait()
+            dn_copy(sd_ref, 1, slice(0, NT), slot).wait()
 
         gu_start(0, 0)
 
@@ -369,8 +383,9 @@
             token = tok_ref[slot]
             for s in range(3):
                 recv[0, s * SLOTS + slot] = normed_ref[token, s]
-        for copy in weight_copies:
-            copy.wait()
+        for which in range(3):
+            for part in range(4):
+                weight_copy(which, part).wait()
 
         def chunk(g, carry):
             def arrive(i, carry):
@@ -407,8 +422,8 @@
                     dn_start(0, 0)
 
                 gu_wait(slot)
-                g_all = dot(rows_in[...], wgu[slot, 0])
-                u_all = dot(rows_in[...], wgu[slot, 1])
+                both = dot(rows_in[...], wgu[slot])
+                g_all, u_all = both[:, :FT], both[:, FT:]
                 n = SLOTS * HALF
                 g0, u0 = g_all[:n], u_all[:n]
                 sigma = 1.0 / (1.0 + jnp.exp(-g0))
@@ -434,7 +449,7 @@
                     gu_start(0, 0)
 
                 dn_wait(slot)
-                part = dot(hidden[:, :FH], wdn[slot, 0]) + dot(hidden[:, FH:], wdn[slot, 1])
+                part = dot(hidden[...], wdn[slot])
                 for q in range(NT // LANES):
                     for half in (0, 1):
                         first = q * LANES + half * 128
@@ -470,8 +485,8 @@
         pltpu.VMEM((ROWS, D), BF),
         pltpu.VMEM((ROWS, 2 * FH), BF),
         pltpu.VMEM((2, ROWS * FOLD, 128), F32),
-        pltpu.VMEM((2, 2, D, FT), BF),
-        pltpu.VMEM((2, 2, FH, NT), BF),
+        pltpu.VMEM((2, D, 2 * FT), BF),
+        pltpu.VMEM((2, 2 * FH, NT), BF),
     )
     back[0] = recv[0]
 
@@ -552,8 +567,8 @@
             pltpu.VMEM(tiles, BF),
             pltpu.VMEM((3, 2, TOK * FOLD, 128), F32),
             dma((6,)),
-            dma((3,)),
-            dma((3,)),
+            dma((12,)),
+            dma((12,)),
             dma((15,)),
             dma((SEQ,)),
             dma((15,)),

time: 228 us -> 233 us (1.022); the launches traced: 224 us -> 232 us
  Pallas kernels: 219 us -> 227 us
    pallas_call x1, Pallas kernels: 219 us -> 227 us  [layer(): pl.pallas_call(layer_kernel, out_shape=(jax.ShapeDtypeStruct((3, TOK, D),...]
where the time goes in v3:
time: 233 us; the launch traced here: 232 us
  Pallas kernels  227 us (97%)
  local copies, waits for them, and re-layouts  3.77 us (2%)
    pallas_call x1, Pallas kernels, layer(): pl.pallas_call(layer_kernel, out_shape=(jax.ShapeDtypeStruct((3, TOK, D),...  227 us

profile of v3, /device:TPU:2, one launch (start us, length us, event | category | flops | bytes accessed | tf_op | source)
XLA Modules:
  0.0 232.2 jit_solution(12238868450727364750)
XLA Ops:
  0.7 0.8 reshape.160
  1.4 0.2 convert_reduce_fusion
  1.6 0.0 copy-start
  1.7 0.1 select_reduce_fusion
  1.8 0.6 broadcast_add_fusion.tok_ref
  2.3 0.0 copy-done
  2.3 226.8 %layer.1 = (bf16[3,16,4096]{2,1,0:T(8,128)(2,1)}, f32[2,16]{1,0:T(2,128)}, bf16[1,4096,768]{2,1,0:T(8,128)(2,1)}, bf16[1,4096,768]{2,1,0:T(8,128)(2,1)}, bf16[1,768,4096]{2,1,0:T(8,128)(2,1)}) custom-call(s32[192]{0:T(256)} %broadcast_add_fusion.tok_ref, s32[128]{0:T(128)} %copy-done, f32[8,16]{1,0:T(8,128)} %bitcast.4, bf16[3,128,512]{2,1,0:T(8,128)(2,1)} %q_hbm.1, ...), custom_call_target="tpu_custom_call" | custom-call | tf_op jit(solution)/shard_map/layer/pallas_call | solution.py:541
  229.2 1.8 copy.15
  231.0 1.2 copy.16
  (1 shorter events, 0.0 us)
Async XLA Ops:
  1.6 0.7 copy-start

commit v4 on v3

v4 whole, which is shorter than its diff:
```python
import math

import jax
import jax.numpy as jnp
from jax import lax
from jax.experimental import pallas as pl
from jax.experimental.pallas import tpu as pltpu
from jax.sharding import PartitionSpec as P

HD = 128
EPS = 1e-06
MESH = pl.DeviceIdType.MESH
BF = jnp.bfloat16
F32 = jnp.float32

SEQ = 16
KEYS = 128
TOK = 16
D = 4096
LANES = 256
FOLD = D // LANES
CHIPS = 64
SLOTS = 3
VECS = 3 * SLOTS
FH = 768
ROWS = CHIPS * VECS
FT = 256
NT = 512


def dot(a, b):
    return jnp.dot(a, b, preferred_element_type=F32)


def dot_nt(a, b):
    return lax.dot_general(a, b, (((1,), (1,)), ((), ())), preferred_element_type=F32)


def place():
    seq, ex = lax.axis_index("seq"), lax.axis_index("exp")
    return lax.div(seq, 4), lax.rem(seq, 4), lax.div(ex, 2), lax.rem(ex, 2)


def peer(i, sign):
    z, x, y, core = place()
    dy = lax.rem(i, 4)
    dz = lax.rem(lax.div(i, 16) + dy, 4)
    dx = lax.rem(lax.rem(lax.div(i, 4), 4) + dy, 4)
    if sign < 0:
        dz, dx, dy = 4 - dz, 4 - dx, 4 - dy
    return (lax.rem(z + dz, 4) * 4 + lax.rem(x + dx, 4), lax.rem(y + dy, 4) * 2 + core)


def remote(src, dst, ssem, rsem, device):
    return pltpu.make_async_remote_copy(
        src_ref=src, dst_ref=dst, send_sem=ssem, recv_sem=rsem, device_id=device, device_id_type=MESH
    )


def greet(i, carry):
    barrier = pltpu.get_barrier_semaphore()
    pl.semaphore_signal(barrier, inc=1, device_id=peer(i, 1), device_id_type=MESH)
    return carry


def attend_kernel(
    tok_ref,
    q_hbm,
    k_hbm,
    v_hbm,
    res_hbm,
    gain_hbm,
    wo_hbm,
    wg_ref,
    wu_ref,
    wd_ref,
    summed_ref,
    recv,
    sg_ref,
    su_ref,
    sd_ref,
    q_ref,
    res_ref,
    gain_ref,
    normed_ref,
    stage,
    kb,
    vb,
    sib_send,
    sib_recv,
    own,
    y_send,
    y_recv,
    send,
    in_sem,
    w_send,
    w_recv,
    k_send,
    k_recv,
    v_send,
    v_recv,
    s_send,
    s_recv,
    ys_send,
    ys_recv,
    send_sem,
    recv_sem,
):
    seq = lax.axis_index("seq")
    ex = lax.axis_index("exp")
    z, x = lax.div(seq, 4), lax.rem(seq, 4)
    y, core = lax.div(ex, 2), lax.rem(ex, 2)
    sibling = (seq, y * 2 + (1 - core))
    scale = 1.0 / math.sqrt(HD)
    order = (1, 3, 2)

    def z_peer(d):
        return (lax.rem(z + d, 4) * 4 + x, ex)

    def x_peer(d):
        return (z * 4 + lax.rem(x + d, 4), ex)

    def y_peer(d):
        return (seq, lax.rem(y + d, 4) * 2 + core)

    barrier = pltpu.get_barrier_semaphore()
    pl.semaphore_signal(barrier, inc=1, device_id=sibling, device_id_type=MESH)

    lax.fori_loop(1, CHIPS, greet, 0)
    k_in = pltpu.make_async_copy(k_hbm, kb.at[seq], in_sem.at[0])
    v_in = pltpu.make_async_copy(v_hbm, vb.at[seq], in_sem.at[1])
    q_in = pltpu.make_async_copy(q_hbm, q_ref, in_sem.at[2])
    res_in = pltpu.make_async_copy(res_hbm, res_ref, in_sem.at[3])
    gain_in = pltpu.make_async_copy(gain_hbm, gain_ref, in_sem.at[4])
    for copy in (k_in, v_in, q_in, res_in, gain_in):
        copy.start()
    k_in.wait()
    v_in.wait()
    pl.semaphore_wait(barrier, CHIPS)

    def weight_copy(which, part):
        source = (wg_ref, wu_ref, wd_ref)[which]
        place = (sg_ref, su_ref, sd_ref)[which]
        count = (D, D, FH)[which] // 4
        rows = pl.ds(pl.multiple_of(part * count, count), count)
        number = which * 4 + part
        return remote(source.at[0, rows, :], place.at[0, rows, :], w_send.at[number], w_recv.at[number], sibling)

    def k_copy(origin, number, peer):
        return remote(kb.at[origin], kb.at[origin], k_send.at[number], k_recv.at[origin], peer)

    def v_copy(origin, number, peer):
        return remote(vb.at[origin], vb.at[origin], v_send.at[number], v_recv.at[origin], peer)

    for d in order:
        k_copy(seq, d - 1, z_peer(d)).start()
        v_copy(seq, d - 1, x_peer(d)).start()
    for d in order:
        k_copy(seq, 3 + d - 1, x_peer(d)).start()
        v_copy(seq, 3 + d - 1, z_peer(d)).start()
    for part in range(4):
        weight_copy(0, part).start()

    def attend(qs, qc, scores, slopes, att, wo):
        wo_copy = pltpu.make_async_copy(wo_hbm, wo, in_sem.at[5])
        wo_copy.start(priority=1)
        q_in.wait()
        for h in range(4):
            for s in range(3):
                qs[s, h * 128 : (h + 1) * 128, :] = q_ref[s, :, h * 128 : (h + 1) * 128]
        for t in (1, 2):
            qc[t - 1, :, :HD] = qs[t]
            qc[t - 1, :, HD:] = qs[0]

        for d in order:
            from_z = lax.rem(z + d, 4) * 4 + x
            from_x = z * 4 + lax.rem(x + d, 4)
            k_copy(from_z, 0, z_peer(d)).wait_recv()
            for e in order:
                k_copy(from_z, 3 * (d + 1) + e - 1, x_peer(e)).start()
            v_copy(from_x, 0, x_peer(d)).wait_recv()
            for e in order:
                v_copy(from_x, 3 * (d + 1) + e - 1, z_peer(e)).start()

        for part in range(4):
            weight_copy(1, part).start()

        for dz in (0,) + order:
            c = lax.rem(z + dz, 4)
            for e in (1, 2, 3):
                k_copy(c * 4 + lax.rem(x + e, 4), 0, x_peer(e)).wait_recv()
            kc = kb[pl.ds(c * 4, 4)]
            k0 = kc[:, 0].reshape(512, HD)
            scores[c] = dot_nt(qs[0], k0) * scale
            for t in (1, 2):
                kt = kc[:, t].reshape(512, HD)
                slopes[t - 1, c] = dot_nt(qc[t - 1], jnp.concatenate([k0, kt], axis=1)) * scale

        for d in order:
            for e in (0, 1, 2, 3):
                origin = lax.rem(z + d, 4) * 4 + lax.rem(x + e, 4)
                v_copy(origin, 0, z_peer(d)).wait_recv()

        def head(h, carry):
            rows = pl.ds(pl.multiple_of(h * 128, 128), 128)
            top = jnp.max(scores[0, rows, :], axis=1, keepdims=True)
            for c in (1, 2, 3):
                top = jnp.maximum(top, jnp.max(scores[c, rows, :], axis=1, keepdims=True))
            norm = jnp.zeros((128, 1), F32)
            r1 = jnp.zeros((128, 1), F32)
            r2 = jnp.zeros((128, 1), F32)
            acc = jnp.zeros((128, 3 * HD), F32)
            mixed = jnp.zeros((256, HD), F32)
            for c in range(4):
                p = jnp.exp(scores[c, rows, :] - top).astype(BF)
                pf = p.astype(F32)
                w1 = (pf * slopes[0, c, rows, :]).astype(BF)
                w2 = (pf * slopes[1, c, rows, :]).astype(BF)
                norm += jnp.sum(pf, axis=1, keepdims=True)
                r1 += jnp.sum(w1.astype(F32), axis=1, keepdims=True)
                r2 += jnp.sum(w2.astype(F32), axis=1, keepdims=True)
                v0 = vb[4 * c : 4 * c + 4, 0].reshape(512, HD)
                v1 = vb[4 * c : 4 * c + 4, 1].reshape(512, HD)
                v2 = vb[4 * c : 4 * c + 4, 2].reshape(512, HD)
                acc += dot(p, jnp.concatenate([v0, v1, v2], axis=1))
                mixed += dot(jnp.concatenate([w1, w2], axis=0), v0)
            inv = 1.0 / norm
            main = acc[:, :HD] * inv
            t1 = (mixed[:128] + acc[:, HD : 2 * HD]) * inv - (r1 * inv) * main
            t2 = (mixed[128:] + acc[:, 2 * HD :]) * inv - (r2 * inv) * main
            att[0, :, rows] = main.astype(BF)
            att[1, :, rows] = t1.astype(BF)
            att[2, :, rows] = t2.astype(BF)
            return carry

        lax.fori_loop(0, 4, head, 0)

        wo_copy.wait()

        def block_rows(parity):
            parts = []
            for d in range(4):
                j = lax.rem(y + d, 4) * 2 + parity
                rows = pl.ds(pl.multiple_of(j * TOK, TOK), TOK)
                for s in range(3):
                    parts.append(att[s, rows, :])
            return jnp.concatenate(parts, axis=0)

        sib_rows = block_rows(1 - core)
        sib_copies = []
        for n in range(4):
            sib_send[n] = dot(sib_rows, wo[:, n * 1024 : (n + 1) * 1024]).astype(BF)
            copy = remote(sib_send.at[n], sib_recv.at[n], s_send.at[n], s_recv.at[n], sibling)
            copy.start()
            sib_copies.append(copy)
        own_rows = block_rows(core)
        y_copies = []
        for n in range(4):
            lanes = slice(n * 1024, (n + 1) * 1024)
            product = dot(own_rows, wo[:, lanes])
            sib_copies[n].wait_recv()
            both = product + sib_recv[n].astype(F32)
            own[:, lanes] = both[:48]
            for d in order:
                y_send[n, d - 1] = both[48 * d : 48 * (d + 1)].astype(BF)
                copy = remote(
                    y_send.at[n, d - 1], y_recv.at[n, d - 1], ys_send.at[n, d - 1], ys_recv.at[n, d - 1], y_peer(d)
                )
                copy.start()
                y_copies.append(copy)
        for part in range(4):
            weight_copy(2, part).start()
        res_in.wait()
        for n in range(4):
            for d in (1, 2, 3):
                y_copies[n * 3 + order.index(d)].wait_recv()
            lanes = slice(n * 1024, (n + 1) * 1024)
            part = own[:, lanes]
            for d in (1, 2, 3):
                part += y_recv[n, d - 1].astype(F32)
            for s in range(3):
                summed_ref[s, :, lanes] = part[16 * s : 16 * (s + 1)] + res_ref[s, :, lanes].astype(F32)
        for d in order:
            k_copy(seq, d - 1, z_peer(d)).wait_send()
            v_copy(seq, d - 1, x_peer(d)).wait_send()
        for number in range(3, 15):
            k_copy(seq, number, x_peer(1)).wait_send()
            v_copy(seq, number, z_peer(1)).wait_send()
        for copy in sib_copies + y_copies:
            copy.wait_send()

    pl.run_scoped(
        attend,
        pltpu.VMEM((3, 512, HD), BF),
        pltpu.VMEM((2, 512, 2 * HD), BF),
        pltpu.VMEM((4, 512, 512), F32),
        pltpu.VMEM((2, 4, 512, 512), F32),
        pltpu.VMEM((3, KEYS, 512), BF),
        pltpu.VMEM((512, D), BF),
    )

    gain_in.wait()
    main_sum = summed_ref[0]
    recip = lax.rsqrt(jnp.mean(main_sum * main_sum, axis=-1, keepdims=True) + EPS)
    normed_ref[TOK] = jnp.zeros((3, FOLD, LANES), BF)
    for s in range(3):
        if s == 0:
            rows = main_sum * recip * gain_ref[...]
        else:
            inner = jnp.mean(main_sum * summed_ref[s], axis=-1, keepdims=True)
            rows = (summed_ref[s] * recip - main_sum * (recip * recip * recip * inner)) * gain_ref[...]
        for c in range(FOLD):
            for half in (0, 1):
                first = c * LANES + half * 128
                stage[half, pl.ds(c, TOK, stride=FOLD), :] = rows[:, first : first + 128]
        for half in (0, 1):
            normed_ref[:TOK, s, :, half * 128 : half * 128 + 128] = (
                stage[half, : TOK * FOLD].reshape(TOK, FOLD, 128).astype(BF)
            )

    def out_copy(i):
        return remote(send.at[i], recv.at[i], send_sem.at[i], recv_sem.at[i], peer(i, 1))

    def fill(i):
        for slot in range(SLOTS):
            token = tok_ref[i * SLOTS + slot]
            for s in range(3):
                send[i, s * SLOTS + slot] = normed_ref[token, s]

    def dispatch(i, carry):
        fill(i)
        out_copy(i).start()
        return carry

    lax.fori_loop(1, CHIPS, dispatch, 0)

    fill(0)
    stay = pltpu.make_async_copy(send.at[0], recv.at[0], in_sem.at[6])
    stay.start()
    for which in range(3):
        for part in range(4):
            weight_copy(which, part).wait()
    stay.wait()

    def collect(i, carry):
        out_copy(i).wait()
        return carry

    lax.fori_loop(1, CHIPS, collect, 0)


def attend(tok, q, k, v, residual, gain, w_out, w_gate, w_up, w_down):
    smem = pl.BlockSpec(memory_space=pltpu.SMEM)
    vmem = pl.BlockSpec(memory_space=pltpu.VMEM)
    hbm = pl.BlockSpec(memory_space=pltpu.HBM)
    dma = pltpu.SemaphoreType.DMA
    tiles = (CHIPS, VECS, FOLD, LANES)
    return pl.pallas_call(
        attend_kernel,
        out_shape=(
            jax.ShapeDtypeStruct((3, TOK, D), F32),
            jax.ShapeDtypeStruct(tiles, BF),
            jax.ShapeDtypeStruct(w_gate.shape, BF),
            jax.ShapeDtypeStruct(w_up.shape, BF),
            jax.ShapeDtypeStruct(w_down.shape, BF),
        ),
        in_specs=[smem] + [hbm] * 9,
        out_specs=(vmem, hbm, hbm, hbm, hbm),
        scratch_shapes=[
            pltpu.VMEM((3, KEYS, 512), BF),
            pltpu.VMEM((3, TOK, D), BF),
            pltpu.VMEM((1, D), F32),
            pltpu.VMEM((TOK + 1, 3, FOLD, LANES), BF),
            pltpu.VMEM((2, TOK * FOLD, 128), F32),
            pltpu.VMEM((SEQ, 3, KEYS, HD), BF),
            pltpu.VMEM((SEQ, 3, KEYS, HD), BF),
            pltpu.VMEM((4, 192, 1024), BF),
            pltpu.VMEM((4, 192, 1024), BF),
            pltpu.VMEM((48, D), F32),
            pltpu.VMEM((4, 3, 48, 1024), BF),
            pltpu.VMEM((4, 3, 48, 1024), BF),
            pltpu.VMEM(tiles, BF),
            dma((7,)),
            dma((12,)),
            dma((12,)),
            dma((15,)),
            dma((SEQ,)),
            dma((15,)),
            dma((SEQ,)),
            dma((4,)),
            dma((4,)),
            dma((4, 3)),
            dma((4, 3)),
            dma((CHIPS,)),
            dma((CHIPS,)),
        ],
        compiler_params=pltpu.CompilerParams(
            collective_id=0, has_side_effects=True, vmem_limit_bytes=56 * 2**20
        ),
        name="attend",
    )(tok, q, k, v, residual, gain, w_out, w_gate, w_up, w_down)


def expert_kernel(
    recv_hbm, wg_ref, wu_ref, wd_ref, sg_ref, su_ref, sd_ref, done_ref, recv, rows_in, hidden, stage, wgu, wdn, in_sem, gu_sem, dn_sem
):
    recv_in = pltpu.make_async_copy(recv_hbm, recv, in_sem)
    recv_in.start()

    def gu_copy(source, which, lanes, slot):
        place = wgu.at[slot, :, which * FT : (which + 1) * FT]
        return pltpu.make_async_copy(source.at[0, :, lanes], place, gu_sem.at[slot, which])

    def dn_copy(source, which, lanes, slot):
        place = wdn.at[slot, which * FH : (which + 1) * FH, :]
        return pltpu.make_async_copy(source.at[0, :, lanes], place, dn_sem.at[slot, which])

    def gu_start(t, slot):
        lanes = pl.ds(pl.multiple_of(lax.rem(t, 3) * FT, FT), FT)

        def go(gate, up):
            gu_copy(gate, 0, lanes, slot).start(priority=1)
            gu_copy(up, 1, lanes, slot).start(priority=1)

        @pl.when(t < 3)
        def _():
            go(wg_ref, wu_ref)

        @pl.when(t >= 3)
        def _():
            go(sg_ref, su_ref)

    def gu_wait(slot):
        gu_copy(wg_ref, 0, slice(0, FT), slot).wait()
        gu_copy(wu_ref, 1, slice(0, FT), slot).wait()

    def dn_start(n, slot):
        lanes = pl.ds(pl.multiple_of(n * NT, NT), NT)
        dn_copy(wd_ref, 0, lanes, slot).start(priority=1)
        dn_copy(sd_ref, 1, lanes, slot).start(priority=1)

    def dn_wait(slot):
        dn_copy(wd_ref, 0, slice(0, NT), slot).wait()
        dn_copy(sd_ref, 1, slice(0, NT), slot).wait()

    gu_start(0, 0)
    recv_in.wait()

    def unfold(m, carry):
        v, part = lax.div(m, 4), lax.rem(m, 4)
        tiles = recv[pl.ds(part * 16, 16), v].astype(F32).reshape(16 * FOLD, LANES)
        for half in (0, 1):
            stage[half, : 16 * FOLD] = tiles[:, half * 128 : half * 128 + 128]
        row = pl.multiple_of(v * CHIPS + part * 16, 16)
        for c in range(FOLD):
            for half in (0, 1):
                first = c * LANES + half * 128
                rows_in[pl.ds(row, 16), first : first + 128] = stage[
                    half, pl.ds(c, 16, stride=FOLD), :
                ].astype(BF)
        return carry

    lax.fori_loop(0, 4 * VECS, unfold, 0)

    def gate_up(t, carry):
        slot = lax.rem(t, 2)

        @pl.when(t < 5)
        def _():
            gu_start(t + 1, 1 - slot)

        @pl.when(t == 5)
        def _():
            dn_start(0, 0)

        gu_wait(slot)
        both = dot(rows_in[...], wgu[slot])
        g_all, u_all = both[:, :FT], both[:, FT:]
        n = SLOTS * CHIPS
        g0, u0 = g_all[:n], u_all[:n]
        sigma = 1.0 / (1.0 + jnp.exp(-g0))
        active = g0 * sigma
        slope = sigma * (1.0 + g0 * (1.0 - sigma)) * u0
        lanes = pl.ds(pl.multiple_of(t * FT, FT), FT)
        hidden[:n, lanes] = (active * u0).astype(BF)
        hidden[n : 2 * n, lanes] = (slope * g_all[n : 2 * n] + active * u_all[n : 2 * n]).astype(BF)
        hidden[2 * n :, lanes] = (slope * g_all[2 * n :] + active * u_all[2 * n :]).astype(BF)
        return carry

    lax.fori_loop(0, 6, gate_up, 0)

    def down(n, carry):
        slot = lax.rem(n, 2)

        @pl.when(n < D // NT - 1)
        def _():
            dn_start(n + 1, 1 - slot)

        dn_wait(slot)
        part = dot(hidden[...], wdn[slot])
        for q in range(NT // LANES):
            for half in (0, 1):
                first = q * LANES + half * 128
                stage[half, pl.ds(n * (NT // LANES) + q, ROWS, stride=FOLD), :] = part[
                    :, first : first + 128
                ]
        return carry

    lax.fori_loop(0, D // NT, down, 0)

    def fold(v, carry):
        for part in range(4):
            row = pl.multiple_of((v * CHIPS + part * 16) * FOLD, 256)
            for half in (0, 1):
                done_ref[part * 16 : part * 16 + 16, v, :, half * 128 : half * 128 + 128] = (
                    stage[half, pl.ds(row, 16 * FOLD), :].reshape(16, FOLD, 128).astype(BF)
                )
        return carry

    lax.fori_loop(0, VECS, fold, 0)


def experts(recv, wg, wu, wd, sg, su, sd):
    vmem = pl.BlockSpec(memory_space=pltpu.VMEM)
    hbm = pl.BlockSpec(memory_space=pltpu.HBM)
    dma = pltpu.SemaphoreType.DMA
    tiles = (CHIPS, VECS, FOLD, LANES)
    return pl.pallas_call(
        expert_kernel,
        out_shape=jax.ShapeDtypeStruct(tiles, BF),
        in_specs=[hbm] * 7,
        out_specs=vmem,
        scratch_shapes=[
            pltpu.VMEM(tiles, BF),
            pltpu.VMEM((ROWS, D), BF),
            pltpu.VMEM((ROWS, 2 * FH), BF),
            pltpu.VMEM((2, ROWS * FOLD, 128), F32),
            pltpu.VMEM((2, D, 2 * FT), BF),
            pltpu.VMEM((2, 2 * FH, NT), BF),
            dma,
            dma((2, 2)),
            dma((2, 2)),
        ],
        compiler_params=pltpu.CompilerParams(vmem_limit_bytes=56 * 2**20),
        name="experts",
    )(recv, wg, wu, wd, sg, su, sd)


def combine_kernel(
    pos_ref, gains_ref, done_ref, summed_ref, res_ref, out_ref, probe_ref, back, total, own_sem, bsend_sem, brecv_sem
):
    barrier = pltpu.get_barrier_semaphore()
    lax.fori_loop(1, CHIPS, greet, 0)
    stay = pltpu.make_async_copy(done_ref.at[0], back.at[0], own_sem)
    stay.start()
    pl.semaphore_wait(barrier, CHIPS - 1)

    def back_copy(i):
        return remote(done_ref.at[i], back.at[i], bsend_sem.at[i], brecv_sem.at[i], peer(i, -1))

    def give_back(i, carry):
        back_copy(i).start()
        return carry

    lax.fori_loop(1, CHIPS, give_back, 0)
    stay.wait()

    def collect(i, carry):
        back_copy(i).wait()
        return carry

    lax.fori_loop(1, CHIPS, collect, 0)

    def combine(tok, carry):
        sums = [jnp.zeros((FOLD, LANES), F32) for _ in range(3)]
        for r in range(8):
            where = pos_ref[r * TOK + tok]
            chip, slot = lax.div(where, SLOTS), lax.rem(where, SLOTS)
            weight = gains_ref[r, tok]
            for s in range(3):
                sums[s] += weight * back[chip, s * SLOTS + slot].astype(F32)
        row = pl.ds(pl.multiple_of(tok * FOLD, FOLD), FOLD)
        for s in range(3):
            for half in (0, 1):
                total[s, half, row, :] = sums[s][:, half * 128 : half * 128 + 128]
        return carry

    lax.fori_loop(0, TOK, combine, 0)
    probes = [jnp.zeros((TOK, 128), F32) for _ in range(2)]
    for c in range(FOLD):
        for half in (0, 1):
            first = c * LANES + half * 128
            lanes = slice(first, first + 128)
            for s in range(3):
                value = summed_ref[s, :, lanes] + total[s, half, pl.ds(c, TOK, stride=FOLD), :]
                out_ref[s, :, lanes] = value.astype(BF)
                if s:
                    probes[s - 1] += value * res_ref[s, :, lanes].astype(F32)
    diagonal = lax.broadcasted_iota(jnp.int32, (TOK, 128), 0) == lax.broadcasted_iota(jnp.int32, (TOK, 128), 1)
    for t in range(2):
        mean = jnp.sum(probes[t], axis=1, keepdims=True) * (1.0 / D)
        flat = jnp.sum(jnp.where(diagonal, mean, 0.0), axis=0, keepdims=True)
        probe_ref[t : t + 1, :] = flat[:, :TOK]


def give_back(pos, gains, done, summed, residual):
    smem = pl.BlockSpec(memory_space=pltpu.SMEM)
    vmem = pl.BlockSpec(memory_space=pltpu.VMEM)
    dma = pltpu.SemaphoreType.DMA
    return pl.pallas_call(
        combine_kernel,
        out_shape=(
            jax.ShapeDtypeStruct((3, TOK, D), BF),
            jax.ShapeDtypeStruct((2, TOK), F32),
        ),
        in_specs=[smem] * 2 + [vmem] * 3,
        out_specs=(vmem, vmem),
        scratch_shapes=[
            pltpu.VMEM((CHIPS, VECS, FOLD, LANES), BF),
            pltpu.VMEM((3, 2, TOK * FOLD, 128), F32),
            dma,
            dma((CHIPS,)),
            dma((CHIPS,)),
        ],
        compiler_params=pltpu.CompilerParams(
            collective_id=1, has_side_effects=True, vmem_limit_bytes=40 * 2**20
        ),
        name="give_back",
    )(pos, gains, done, summed, residual)


def plan(routes):
    seq, ex = lax.axis_index("seq"), lax.axis_index("exp")
    z, x, y = seq // 4, seq % 4, ex // 2
    flat = routes.T.reshape(-1)
    count = flat.shape[0]
    order = jnp.arange(count)
    earlier = (flat[:, None] == flat[None, :]) & (order[None, :] < order[:, None])
    slot = jnp.sum(earlier.astype(jnp.int32), axis=1)
    dz = (flat // 16 - z) % 4
    dx = (flat // 4 % 4 - x) % 4
    dy = (flat % 4 - y) % 4
    number = (dz - dy) % 4 * 16 + (dx - dy) % 4 * 4 + dy
    pos = number * SLOTS + slot
    hit = (jnp.arange(CHIPS * SLOTS)[:, None] == pos[None, :]).astype(jnp.int32)
    tok = TOK + jnp.sum(hit * (order % TOK - TOK)[None, :], axis=1)
    return tok.astype(jnp.int32), pos.astype(jnp.int32)


def shards(
    queries,
    key_rows,
    value_rows,
    residual,
    w_out,
    norm_gain,
    w_gate,
    w_up,
    w_down,
    routes,
    route_gain,
):
    tok, pos = plan(routes)
    summed, recv, sg, su, sd = attend(
        tok, queries, key_rows, value_rows, residual, norm_gain[None, :], w_out, w_gate, w_up, w_down
    )
    done = experts(recv, w_gate, w_up, w_down, sg, su, sd)
    return give_back(pos, route_gain.T, done, summed, residual)


def solution(mesh):
    return jax.shard_map(
        shards,
        mesh=mesh,
        in_specs=(
            P(None, "seq", "exp"),
            P(None, "seq", "exp"),
            P(None, "seq", "exp"),
            P(None, ("seq", "exp"), None),
            P("exp", None),
            P(),
            P(("seq", "exp"), None, None),
            P(("seq", "exp"), None, None),
            P(("seq", "exp"), None, None),
            P(("seq", "exp"), None),
            P(("seq", "exp"), None),
        ),
        out_specs=(P(None, ("seq", "exp"), None), P(None, ("seq", "exp"))),
        check_vma=False,
    )
```

time: 233 us -> 231 us (level); the launches traced: 232 us -> 227 us
  Pallas kernels: 227 us -> 221 us
    pallas_call x1 -> x3, Pallas kernels: 227 us -> 221 us  [the longest x1 119 us: attend(): pl.pallas_call(attend_kernel, out_shape=(jax.ShapeDtypeStruct((3, TOK, D)...]
where the time goes in v4:
time: 231 us; the launch traced here: 227 us
  Pallas kernels  221 us (96%)
  local copies, waits for them, and re-layouts  4.42 us (2%)
    pallas_call x1, Pallas kernels, attend(): pl.pallas_call(attend_kernel, out_shape=(jax.ShapeDtypeStruct((3, TOK, D)...  119 us
    pallas_call x1, Pallas kernels, give_back(): pl.pallas_call(combine_kernel, out_shape=(jax.ShapeDtypeStruct((3, TOK, D...  65.5 us
    pallas_call x1, Pallas kernels, experts(): pl.pallas_call(expert_kernel, out_shape=jax.ShapeDtypeStruct(tiles, BF),...  35.8 us

profile of v4, /device:TPU:2, one launch (start us, length us, event | category | flops | bytes accessed | tf_op | source)
XLA Modules:
  0.0 226.6 jit_solution(14847959253776612009)
XLA Ops:
  0.7 0.8 reshape.156
  1.4 0.2 convert_reduce_fusion
  1.7 0.1 select_reduce_fusion
  1.8 0.6 broadcast_add_fusion.tok_ref
  2.3 119.3 %attend.1 = (f32[3,16,4096]{2,1,0:T(8,128)}, bf16[64,9,16,256]{3,2,1,0:T(8,128)(2,1)}, bf16[1,4096,768]{2,1,0:T(8,128)(2,1)}, bf16[1,4096,768]{2,1,0:T(8,128)(2,1)}, bf16[1,768,4096]{2,1,0:T(8,128)(2,1)}) custom-call(s32[192]{0:T(256)} %broadcast_add_fusion.tok_ref, bf16[3,128,512]{2,1,0:T(8,128)(2,1)} %q_hbm.1, bf16[3,128,128]{2,1,0:T(8,128)(2,1)} %k_hbm.1, ...), custom_call_target="tpu_custom_call" | custom-call | tf_op jit(solution)/shard_map/attend/pallas_call | solution.py:358
  121.7 0.0 copy-start.1
  121.7 0.0 copy-start.2
  121.7 0.0 copy-start.3
  121.7 35.8 %experts.1.done_ref = bf16[64,9,16,256]{3,2,1,0:T(8,128)(2,1)} custom-call(bf16[64,9,16,256]{3,2,1,0:T(8,128)(2,1)} %get-tuple-element.7.recv_hbm, bf16[1,4096,768]{2,1,0:T(8,128)(2,1)} %wg_ref.3, bf16[1,4096,768]{2,1,0:T(8,128)(2,1)} %wu_ref.3, bf16[1,768,4096]{2,1,0:T(8,128)(2,1)} %wd_ref.3, bf16[1,4096,768]{2,1,0:T(8,128)(2,1)} %get-tuple-element.8.sg_ref, ...), custom_call_target="tpu_custom_call" | custom-call | tf_op jit(solution)/shard_map/experts/pallas_call | solution.py:528
  157.5 0.0 copy-done.1
  157.5 0.0 copy-done.2
  157.5 0.0 copy-done.3
  157.5 0.0 copy-start
  157.5 2.3 %copy-done = bf16[64,9,16,256]{3,2,1,0:T(8,128)(2,1)S(1)} copy-done((bf16[64,9,16,256]{3,2,1,0:T(8,128)(2,1)S(1)}, bf16[64,9,16,256]{3,2,1,0:T(8,128)(2,1)}, u32[]{:S(2)}) %copy-start) | copy-done | bytes 4718616
  159.8 65.5 %give_back.1 = (bf16[3,16,4096]{2,1,0:T(8,128)(2,1)S(1)}, f32[2,16]{1,0:T(2,128)S(1)}) custom-call(s32[128]{0:T(128)S(1)} %get-tuple-element.13.pos_ref, f32[8,16]{1,0:T(8,128)S(1)} %bitcast.3, bf16[64,9,16,256]{3,2,1,0:T(8,128)(2,1)S(1)} %copy-done, f32[3,16,4096]{2,1,0:T(8,128)S(1)} %copy-done.2, bf16[3,16,4096]{2,1,0:T(8,128)(2,1)S(1)} %copy-done.1), custom_call_target="tpu_custom_call" | custom-call | tf_op jit(solution)/shard_map/give_back/pallas_call | solution.py:610
  225.3 0.7 copy.15
  226.1 0.6 copy.16
  (1 shorter events, 0.0 us)
Async XLA Ops:
  121.7 35.8 %copy-start.1 = (bf16[3,16,4096]{2,1,0:T(8,128)(2,1)S(1)}, bf16[3,16,4096]{2,1,0:T(8,128)(2,1)}, u32[]{:S(2)}) copy-start(bf16[3,16,4096]{2,1,0:T(8,128)(2,1)} %res_ref.1) | copy-start | bytes 1179652
  121.7 35.8 %copy-start.2 = (f32[3,16,4096]{2,1,0:T(8,128)S(1)}, f32[3,16,4096]{2,1,0:T(8,128)}, u32[]{:S(2)}) copy-start(f32[3,16,4096]{2,1,0:T(8,128)} %get-tuple-element.11.summed_ref) | copy-start | bytes 2359300
  121.7 35.8 %copy-start.3 = (f32[16,8]{0,1:T(8,128)S(1)}, f32[16,8]{0,1:T(8,128)}, u32[]{:S(2)}) copy-start(f32[16,8]{0,1:T(8,128)} %param.21) | copy-start | bytes 1540
  157.5 2.3 %copy-start = (bf16[64,9,16,256]{3,2,1,0:T(8,128)(2,1)S(1)}, bf16[64,9,16,256]{3,2,1,0:T(8,128)(2,1)}, u32[]{:S(2)}) copy-start(bf16[64,9,16,256]{3,2,1,0:T(8,128)(2,1)} %experts.1.done_ref) | copy-start | bytes 14155780

commit v5 on v3

--- a/solution.py
+++ b/solution.py
@@ -108,10 +108,9 @@
         return (seq, lax.rem(y + d, 4) * 2 + core)
 
     def peer(i, sign):
-        iz = lax.div(i, 16)
-        dz = lax.rem(iz, 2) * 2 + lax.div(iz, 2)
-        dx = lax.rem(lax.div(i, 4), 4)
         dy = lax.rem(i, 4)
+        dz = lax.rem(lax.div(i, 16) + dy, 4)
+        dx = lax.rem(lax.rem(lax.div(i, 4), 4) + dy, 4)
         if sign < 0:
             dz, dx, dy = 4 - dz, 4 - dx, 4 - dy
         return (lax.rem(z + dz, 4) * 4 + lax.rem(x + dx, 4), lax.rem(y + dy, 4) * 2 + core)
@@ -160,8 +159,8 @@
     for d in order:
         k_copy(seq, 3 + d - 1, x_peer(d)).start()
         v_copy(seq, 3 + d - 1, z_peer(d)).start()
-    weight_copy(0, 0).start()
-    weight_copy(0, 1).start()
+    for part in range(4):
+        weight_copy(0, part).start()
 
     def attend(qs, qc, scores, slopes, att, wo):
         wo_copy = pltpu.make_async_copy(wo_hbm, wo, in_sem.at[5])
@@ -183,14 +182,14 @@
             v_copy(from_x, 0, x_peer(d)).wait_recv()
             for e in order:
                 v_copy(from_x, 3 * (d + 1) + e - 1, z_peer(e)).start()
-            if d != 2:
-                weight_copy(0, 2 + order.index(d)).start()
+
+        for part in range(4):
+            weight_copy(1, part).start()
 
         for dz in (0,) + order:
             c = lax.rem(z + dz, 4)
             for e in (1, 2, 3):
                 k_copy(c * 4 + lax.rem(x + e, 4), 0, x_peer(e)).wait_recv()
-            weight_copy(1, dz).start()
             kc = kb[pl.ds(c * 4, 4)]
             k0 = kc[:, 0].reshape(512, HD)
             scores[c] = dot_nt(qs[0], k0) * scale
@@ -204,7 +203,6 @@
                 v_copy(origin, 0, z_peer(d)).wait_recv()
 
         def head(h, carry):
-            weight_copy(2, h).start()
             rows = pl.ds(pl.multiple_of(h * 128, 128), 128)
             top = jnp.max(scores[0, rows, :], axis=1, keepdims=True)
             for c in (1, 2, 3):
@@ -271,6 +269,8 @@
                 )
                 copy.start()
                 y_copies.append(copy)
+        for part in range(4):
+            weight_copy(2, part).start()
         res_in.wait()
         for n in range(4):
             for d in (1, 2, 3):
@@ -603,7 +603,7 @@
     dz = (flat // 16 - z) % 4
     dx = (flat // 4 % 4 - x) % 4
     dy = (flat % 4 - y) % 4
-    number = (dz % 2 * 2 + dz // 2) * 16 + dx * 4 + dy
+    number = (dz - dy) % 4 * 16 + (dx - dy) % 4 * 4 + dy
     pos = number * SLOTS + slot
     hit = (jnp.arange(CHIPS * SLOTS)[:, None] == pos[None, :]).astype(jnp.int32)
     tok = TOK + jnp.sum(hit * (order % TOK - TOK)[None, :], axis=1)

time: 233 us -> 195 us (0.84)
  the two profiles are of different devices: /device:TPU:2 before, /device:TPU:4 now
where the time goes in v5:
time: 195 us
  Pallas kernels  189 us (97%)
  local copies, waits for them, and re-layouts  3.77 us (2%)
    pallas_call x1, Pallas kernels, layer(): pl.pallas_call(layer_kernel, out_shape=(jax.ShapeDtypeStruct((3, TOK, D),...  189 us

profile of v5, /device:TPU:4, one launch (start us, length us, event | category | flops | bytes accessed | tf_op | source)
XLA Modules:
  0.0 194.5 jit_solution(2505559776869614644)
XLA Ops:
  0.7 0.8 reshape.156
  1.4 0.2 convert_reduce_fusion
  1.7 0.0 copy-start
  1.7 0.1 select_reduce_fusion
  1.8 0.6 broadcast_add_fusion.tok_ref
  2.4 0.0 copy-done
  2.4 189.2 %layer.1 = (bf16[3,16,4096]{2,1,0:T(8,128)(2,1)}, f32[2,16]{1,0:T(2,128)}, bf16[1,4096,768]{2,1,0:T(8,128)(2,1)}, bf16[1,4096,768]{2,1,0:T(8,128)(2,1)}, bf16[1,768,4096]{2,1,0:T(8,128)(2,1)}) custom-call(s32[192]{0:T(256)} %broadcast_add_fusion.tok_ref, s32[128]{0:T(128)} %copy-done, f32[8,16]{1,0:T(8,128)} %bitcast.4, bf16[3,128,512]{2,1,0:T(8,128)(2,1)} %q_hbm.1, ...), custom_call_target="tpu_custom_call" | custom-call | tf_op jit(solution)/shard_map/layer/pallas_call | solution.py:541
  191.5 1.8 copy.15
  193.3 1.2 copy.16
  (1 shorter events, 0.0 us)
Async XLA Ops:
  1.7 0.7 copy-start

commit v6 on v5

--- a/solution.py
+++ b/solution.py
@@ -68,7 +68,8 @@
     own,
     y_send,
     y_recv,
-    send,
+    send0,
+    send12,
     recv,
     back,
     total,
@@ -161,6 +162,28 @@
         v_copy(seq, 3 + d - 1, z_peer(d)).start()
     for part in range(4):
         weight_copy(0, part).start()
+
+    def y_copy(n, d, group):
+        rows = slice(0, TOK) if group == 0 else slice(TOK, 3 * TOK)
+        return remote(
+            y_send.at[n, d - 1, rows, :],
+            y_recv.at[n, d - 1, rows, :],
+            ys_send.at[n, d - 1, group],
+            ys_recv.at[n, d - 1, group],
+            y_peer(d),
+        )
+
+    def y_sum(group):
+        for n in range(4):
+            for d in (1, 2, 3):
+                y_copy(n, d, group).wait_recv()
+            lanes = slice(n * 1024, (n + 1) * 1024)
+            for s in (0,) if group == 0 else (1, 2):
+                rows = slice(s * TOK, (s + 1) * TOK)
+                part = own[rows, lanes] + res_ref[s, :, lanes].astype(F32)
+                for d in (1, 2, 3):
+                    part += y_recv[n, d - 1, rows, :].astype(F32)
+                summed_ref[s, :, lanes] = part
 
     def attend(qs, qc, scores, slopes, att, wo):
         wo_copy = pltpu.make_async_copy(wo_hbm, wo, in_sem.at[5])
@@ -255,7 +278,6 @@
             copy.start()
             sib_copies.append(copy)
         own_rows = block_rows(core)
-        y_copies = []
         for n in range(4):
             lanes = slice(n * 1024, (n + 1) * 1024)
             product = dot(own_rows, wo[:, lanes])
@@ -264,30 +286,21 @@
             own[:, lanes] = both[:48]
             for d in order:
                 y_send[n, d - 1] = both[48 * d : 48 * (d + 1)].astype(BF)
-                copy = remote(
-                    y_send.at[n, d - 1], y_recv.at[n, d - 1], ys_send.at[n, d - 1], ys_recv.at[n, d - 1], y_peer(d)
-                )
-                copy.start()
-                y_copies.append(copy)
+                y_copy(n, d, 0).start()
+        for n in range(4):
+            for d in order:
+                y_copy(n, d, 1).start()
         for part in range(4):
             weight_copy(2, part).start()
         res_in.wait()
-        for n in range(4):
-            for d in (1, 2, 3):
-                y_copies[n * 3 + order.index(d)].wait_recv()
-            lanes = slice(n * 1024, (n + 1) * 1024)
-            part = own[:, lanes]
-            for d in (1, 2, 3):
-                part += y_recv[n, d - 1].astype(F32)
-            for s in range(3):
-                summed_ref[s, :, lanes] = part[16 * s : 16 * (s + 1)] + res_ref[s, :, lanes].astype(F32)
+        y_sum(0)
         for d in order:
             k_copy(seq, d - 1, z_peer(d)).wait_send()
             v_copy(seq, d - 1, x_peer(d)).wait_send()
         for number in range(3, 15):
             k_copy(seq, number, x_peer(1)).wait_send()
             v_copy(seq, number, z_peer(1)).wait_send()
-        for copy in sib_copies + y_copies:
+        for copy in sib_copies:
             copy.wait_send()
 
     pl.run_scoped(
@@ -300,8 +313,10 @@
         pltpu.VMEM((512, D), BF),
     )
 
-    def out_copy(i):
-        return remote(send.at[i], recv.at[i], send_sem.at[i], recv_sem.at[i], peer(i, 1))
+    def out_copy(i, group):
+        if group == 0:
+            return remote(send0.at[i], recv.at[i, 0:SLOTS], send_sem.at[i, 0], recv_sem.at[i, 0], peer(i, 1))
+        return remote(send12.at[i], recv.at[i, SLOTS:VECS], send_sem.at[i, 1], recv_sem.at[i, 1], peer(i, 1))
 
     def back_copy(i):
         return remote(recv.at[i], back.at[i], bsend_sem.at[i], brecv_sem.at[i], peer(i, -1))
@@ -349,12 +364,14 @@
         main_sum = summed_ref[0]
         recip = lax.rsqrt(jnp.mean(main_sum * main_sum, axis=-1, keepdims=True) + EPS)
         normed_ref[TOK] = jnp.zeros((3, FOLD, LANES), BF)
-        for s in range(3):
+
+        def norm(s):
+            main = summed_ref[0]
             if s == 0:
-                rows = main_sum * recip * gain_ref[...]
+                rows = main * recip * gain_ref[...]
             else:
-                inner = jnp.mean(main_sum * summed_ref[s], axis=-1, keepdims=True)
-                rows = (summed_ref[s] * recip - main_sum * (recip * recip * recip * inner)) * gain_ref[...]
+                inner = jnp.mean(main * summed_ref[s], axis=-1, keepdims=True)
+                rows = (summed_ref[s] * recip - main * (recip * recip * recip * inner)) * gain_ref[...]
             for c in range(FOLD):
                 for half in (0, 1):
                     first = c * LANES + half * 128
@@ -364,32 +381,48 @@
                     stage[half, : TOK * FOLD].reshape(TOK, FOLD, 128).astype(BF)
                 )
 
-        def dispatch(i, carry):
+        def dispatch0(i, carry):
+            for slot in range(SLOTS):
+                send0[i, slot] = normed_ref[tok_ref[i * SLOTS + slot], 0]
+            out_copy(i, 0).start()
+            return carry
+
+        def dispatch12(i, carry):
             for slot in range(SLOTS):
                 token = tok_ref[i * SLOTS + slot]
-                for s in range(3):
-                    send[i, s * SLOTS + slot] = normed_ref[token, s]
+                for s in (1, 2):
+                    send12[i, (s - 1) * SLOTS + slot] = normed_ref[token, s]
 
             @pl.when(i > WINDOW)
             def _():
-                out_copy(i - WINDOW).wait_send()
-
-            out_copy(i).start()
+                out_copy(i - WINDOW, 1).wait_send()
+
+            out_copy(i, 1).start()
             return carry
 
-        lax.fori_loop(1, CHIPS, dispatch, 0)
+        norm(0)
+        lax.fori_loop(1, CHIPS, dispatch0, 0)
+        y_sum(1)
+        norm(1)
+        norm(2)
+        lax.fori_loop(1, CHIPS, dispatch12, 0)
 
         for slot in range(SLOTS):
             token = tok_ref[slot]
             for s in range(3):
                 recv[0, s * SLOTS + slot] = normed_ref[token, s]
+        for n in range(4):
+            for d in order:
+                for group in (0, 1):
+                    y_copy(n, d, group).wait_send()
         for which in range(3):
             for part in range(4):
                 weight_copy(which, part).wait()
 
         def chunk(g, carry):
             def arrive(i, carry):
-                out_copy(i).wait_recv()
+                out_copy(i, 0).wait_recv()
+                out_copy(i, 1).wait_recv()
                 return carry
 
             lax.fori_loop(jnp.where(g == 0, 1, HALF), (g + 1) * HALF, arrive, 0)
@@ -491,9 +524,11 @@
     back[0] = recv[0]
 
     def collect(i, carry):
+        out_copy(i, 0).wait_send()
+
         @pl.when(i >= CHIPS - WINDOW)
         def _():
-            out_copy(i).wait_send()
+            out_copy(i, 1).wait_send()
 
         back_copy(i).wait()
         return carry
@@ -503,7 +538,7 @@
     def combine(tok, carry):
         sums = [jnp.zeros((FOLD, LANES), F32) for _ in range(3)]
         for r in range(8):
-            where = pos_ref[r * TOK + tok]
+            where = pos_ref[r, tok]
             chip, slot = lax.div(where, SLOTS), lax.rem(where, SLOTS)
             weight = gains_ref[r, tok]
             for s in range(3):
@@ -562,7 +597,8 @@
             pltpu.VMEM((48, D), F32),
             pltpu.VMEM((4, 3, 48, 1024), BF),
             pltpu.VMEM((4, 3, 48, 1024), BF),
-            pltpu.VMEM(tiles, BF),
+            pltpu.VMEM((CHIPS, SLOTS, FOLD, LANES), BF),
+            pltpu.VMEM((CHIPS, 2 * SLOTS, FOLD, LANES), BF),
             pltpu.VMEM(tiles, BF),
             pltpu.VMEM(tiles, BF),
             pltpu.VMEM((3, 2, TOK * FOLD, 128), F32),
@@ -575,17 +611,17 @@
             dma((SEQ,)),
             dma((4,)),
             dma((4,)),
-            dma((4, 3)),
-            dma((4, 3)),
-            dma((CHIPS,)),
-            dma((CHIPS,)),
+            dma((4, 3, 2)),
+            dma((4, 3, 2)),
+            dma((CHIPS, 2)),
+            dma((CHIPS, 2)),
             dma((CHIPS,)),
             dma((CHIPS,)),
             dma((2, 2)),
             dma((2, 2)),
         ],
         compiler_params=pltpu.CompilerParams(
-            collective_id=0, has_side_effects=True, vmem_limit_bytes=58 * 2**20
+            collective_id=0, has_side_effects=True, vmem_limit_bytes=50 * 2**20
         ),
         name="layer",
     )(tok, pos, gains, q, k, v, residual, gain, w_out, w_gate, w_up, w_down)
@@ -595,18 +631,18 @@
 def plan(routes):
     seq, ex = lax.axis_index("seq"), lax.axis_index("exp")
     z, x, y = seq // 4, seq % 4, ex // 2
-    flat = routes.T.reshape(-1)
-    count = flat.shape[0]
-    order = jnp.arange(count)
-    earlier = (flat[:, None] == flat[None, :]) & (order[None, :] < order[:, None])
-    slot = jnp.sum(earlier.astype(jnp.int32), axis=1)
-    dz = (flat // 16 - z) % 4
-    dx = (flat // 4 % 4 - x) % 4
-    dy = (flat % 4 - y) % 4
+    mine = routes.T
+    order = jnp.arange(8)[:, None] * TOK + jnp.arange(TOK)[None, :]
+    same = mine[:, :, None, None] == mine[None, None]
+    earlier = same & (order[None, None] < order[:, :, None, None])
+    slot = jnp.sum(earlier.astype(jnp.int32), axis=(2, 3))
+    dz = (mine // 16 - z) % 4
+    dx = (mine // 4 % 4 - x) % 4
+    dy = (mine % 4 - y) % 4
     number = (dz - dy) % 4 * 16 + (dx - dy) % 4 * 4 + dy
     pos = number * SLOTS + slot
-    hit = (jnp.arange(CHIPS * SLOTS)[:, None] == pos[None, :]).astype(jnp.int32)
-    tok = TOK + jnp.sum(hit * (order % TOK - TOK)[None, :], axis=1)
+    hit = (jnp.arange(CHIPS * SLOTS)[:, None, None] == pos[None]).astype(jnp.int32)
+    tok = TOK + jnp.sum(hit * (jnp.arange(TOK) - TOK)[None, None, :], axis=(1, 2))
     return tok.astype(jnp.int32), pos.astype(jnp.int32)
 
 

time: 195 us -> 205 us (1.051)
  the two profiles are of different devices: /device:TPU:4 before, /device:TPU:2 now
where the time goes in v6:
time: 205 us; the launch traced here: 202 us
  Pallas kernels  191 us (93%)
  local copies, waits for them, and re-layouts  6.48 us (3%)
  other arithmetic  4.34 us (2%)
    pallas_call x1, Pallas kernels, layer(): pl.pallas_call(layer_kernel, out_shape=(jax.ShapeDtypeStruct((3, TOK, D),...  191 us
    unnamed x14, local copies, waits for them, and re-layouts  6.48 us

profile of v6, /device:TPU:2, one launch (start us, length us, event | category | flops | bytes accessed | tf_op | source)
XLA Modules:
  0.0 202.5 jit_solution(18276146227477857098)
XLA Ops:
  0.7 0.1 iota_add_fusion
  0.8 3.4 %convert_reduce_fusion = s32[8,16]{1,0:T(8,128)S(1)} fusion(s32[8,16]{1,0:T(8,128)S(1)} %iota_add_fusion, s32[8,16]{1,0:T(8,128)} %bitcast.6), kind=kLoop, calls=%fused_computation | loop fusion | flops 81792 | bytes 1536 | tf_op jit(solution)/shard_map/reduce_sum | solution.py:638
  4.2 0.7 fusion.11.pos_ref
  4.9 0.1 select_reduce_fusion
  5.0 0.0 copy-start
  5.0 1.0 copy-done
  6.0 0.0 copy-start.1
  6.0 1.0 copy-done.1
  7.0 0.0 copy-start.2
  7.0 0.9 copy-done.2
  7.9 0.0 copy-start.3
  7.9 0.9 copy-done.3
  8.8 0.0 copy-start.4
  8.8 0.7 copy-done.4
  9.5 0.0 copy-start.5
  9.5 0.7 copy-done.5
  10.2 190.9 %layer.1 = (bf16[3,16,4096]{2,1,0:T(8,128)(2,1)S(1)}, f32[2,16]{1,0:T(2,128)S(1)}, bf16[1,4096,768]{2,1,0:T(8,128)(2,1)}, bf16[1,4096,768]{2,1,0:T(8,128)(2,1)}, bf16[1,768,4096]{2,1,0:T(8,128)(2,1)}) custom-call(s32[192]{0:T(256)S(1)} %broadcast_add_fusion.tok_ref, s32[8,16]{1,0:T(8,128)S(1)} %fusion.11.pos_ref, f32[8,16]{1,0:T(8,128)S(1)} %bitcast.5, ...), custom_call_target="tpu_custom_call" | custom-call | tf_op jit(solution)/shard_map/layer/pallas_call | solution.py:576
  201.2 0.7 copy.15
  201.9 0.6 copy.16
  (3 shorter events, 0.0 us)
Async XLA Ops:
  5.0 1.0 copy-start
  6.0 1.0 copy-start.1
  7.0 0.9 copy-start.2
  7.9 0.9 copy-start.3
  8.8 0.7 copy-start.4
  9.5 0.7 copy-start.5

commit v7 on v5

--- a/solution.py
+++ b/solution.py
@@ -75,10 +75,8 @@
     in_sem,
     w_send,
     w_recv,
-    k_send,
-    k_recv,
-    v_send,
-    v_recv,
+    kv_send,
+    kv_recv,
     s_send,
     s_recv,
     ys_send,
@@ -147,18 +145,35 @@
         number = which * 4 + part
         return remote(source.at[0, rows, :], place.at[0, rows, :], w_send.at[number], w_recv.at[number], sibling)
 
-    def k_copy(origin, number, peer):
-        return remote(kb.at[origin], kb.at[origin], k_send.at[number], k_recv.at[origin], peer)
-
-    def v_copy(origin, number, peer):
-        return remote(vb.at[origin], vb.at[origin], v_send.at[number], v_recv.at[origin], peer)
-
-    for d in order:
-        k_copy(seq, d - 1, z_peer(d)).start()
-        v_copy(seq, d - 1, x_peer(d)).start()
-    for d in order:
-        k_copy(seq, 3 + d - 1, x_peer(d)).start()
-        v_copy(seq, 3 + d - 1, z_peer(d)).start()
+    sides = (1, 3)
+    kv_sent = []
+
+    def origin(which, da, db):
+        dz, dx = (da, db) if which == 0 else (db, da)
+        return lax.rem(z + dz, 4) * 4 + lax.rem(x + dx, 4)
+
+    def kv_copy(which, source, number, half, device):
+        buf = (kb, vb)[which]
+        if half is None:
+            ref = buf.at[source]
+        else:
+            ref = buf.at[source, :, half * 64 : half * 64 + 64, :]
+        arrival = kv_recv.at[which, source, 1 if half == 1 else 0]
+        return remote(ref, ref, kv_send.at[number], arrival, device)
+
+    def push(which, da, db, half, axis, d):
+        first = (axis == 0) == (which == 0)
+        copy = kv_copy(which, origin(which, da, db), len(kv_sent), half, z_peer(d) if first else x_peer(d))
+        copy.start()
+        kv_sent.append(copy)
+
+    def arrived(which, da, db, half):
+        kv_copy(which, origin(which, da, db), 0, half, z_peer(1)).wait_recv()
+
+    for axis in (0, 1):
+        for which in (0, 1):
+            for d in sides:
+                push(which, 0, 0, None, axis, d)
     for part in range(4):
         weight_copy(0, part).start()
 
@@ -173,23 +188,18 @@
             qc[t - 1, :, :HD] = qs[t]
             qc[t - 1, :, HD:] = qs[0]
 
-        for d in order:
-            from_z = lax.rem(z + d, 4) * 4 + x
-            from_x = z * 4 + lax.rem(x + d, 4)
-            k_copy(from_z, 0, z_peer(d)).wait_recv()
-            for e in order:
-                k_copy(from_z, 3 * (d + 1) + e - 1, x_peer(e)).start()
-            v_copy(from_x, 0, x_peer(d)).wait_recv()
-            for e in order:
-                v_copy(from_x, 3 * (d + 1) + e - 1, z_peer(e)).start()
-
-        for part in range(4):
-            weight_copy(1, part).start()
-
-        for dz in (0,) + order:
+        def cross(which, da):
+            for d in sides:
+                arrived(which, da, d, None)
+                push(which, da, d, 1 if d == 1 else 0, 1, 4 - d)
+
+        def opposite(which, da, db):
+            arrived(which, da, db, 0)
+            arrived(which, da, db, 1)
+
+        def score(dz):
+            opposite(0, dz, 2)
             c = lax.rem(z + dz, 4)
-            for e in (1, 2, 3):
-                k_copy(c * 4 + lax.rem(x + e, 4), 0, x_peer(e)).wait_recv()
             kc = kb[pl.ds(c * 4, 4)]
             k0 = kc[:, 0].reshape(512, HD)
             scores[c] = dot_nt(qs[0], k0) * scale
@@ -197,10 +207,27 @@
                 kt = kc[:, t].reshape(512, HD)
                 slopes[t - 1, c] = dot_nt(qc[t - 1], jnp.concatenate([k0, kt], axis=1)) * scale
 
-        for d in order:
-            for e in (0, 1, 2, 3):
-                origin = lax.rem(z + d, 4) * 4 + lax.rem(x + e, 4)
-                v_copy(origin, 0, z_peer(d)).wait_recv()
+        for d in sides:
+            for which in (0, 1):
+                arrived(which, d, 0, None)
+                push(which, d, 0, 1 if d == 1 else 0, 0, 4 - d)
+                for e in sides:
+                    push(which, d, 0, None, 1, e)
+        for which in (0, 1):
+            cross(which, 0)
+        for which in (0, 1):
+            opposite(which, 2, 0)
+            for e in sides:
+                push(which, 2, 0, None, 1, e)
+        done = 0
+        for da in (1, 3, 2):
+            for which in (0, 1):
+                cross(which, da)
+            score(done)
+            done = da
+        score(done)
+        for da in range(4):
+            opposite(1, da, 2)
 
         def head(h, carry):
             rows = pl.ds(pl.multiple_of(h * 128, 128), 128)
@@ -270,6 +297,8 @@
                 copy.start()
                 y_copies.append(copy)
         for part in range(4):
+            weight_copy(1, part).start()
+        for part in range(4):
             weight_copy(2, part).start()
         res_in.wait()
         for n in range(4):
@@ -281,13 +310,7 @@
                 part += y_recv[n, d - 1].astype(F32)
             for s in range(3):
                 summed_ref[s, :, lanes] = part[16 * s : 16 * (s + 1)] + res_ref[s, :, lanes].astype(F32)
-        for d in order:
-            k_copy(seq, d - 1, z_peer(d)).wait_send()
-            v_copy(seq, d - 1, x_peer(d)).wait_send()
-        for number in range(3, 15):
-            k_copy(seq, number, x_peer(1)).wait_send()
-            v_copy(seq, number, z_peer(1)).wait_send()
-        for copy in sib_copies + y_copies:
+        for copy in kv_sent + sib_copies + y_copies:
             copy.wait_send()
 
     pl.run_scoped(
@@ -569,10 +592,8 @@
             dma((6,)),
             dma((12,)),
             dma((12,)),
-            dma((15,)),
-            dma((SEQ,)),
-            dma((15,)),
-            dma((SEQ,)),
+            dma((40,)),
+            dma((2, SEQ, 2)),
             dma((4,)),
             dma((4,)),
             dma((4, 3)),

time: 195 us -> 192 us (0.985)
  Pallas kernels: 189 us -> 186 us
    pallas_call x1, Pallas kernels: 189 us -> 186 us  [layer(): pl.pallas_call(layer_kernel, out_shape=(jax.ShapeDtypeStruct((3, TOK, D),...]
where the time goes in v7:
time: 192 us; the launch traced here: 191 us
  Pallas kernels  186 us (97%)
  local copies, waits for them, and re-layouts  3.77 us (2%)
    pallas_call x1, Pallas kernels, layer(): pl.pallas_call(layer_kernel, out_shape=(jax.ShapeDtypeStruct((3, TOK, D),...  186 us

profile of v7, /device:TPU:4, one launch (start us, length us, event | category | flops | bytes accessed | tf_op | source)
XLA Modules:
  0.0 191.5 jit_solution(17928501683301184787)
XLA Ops:
  0.7 0.8 reshape.156
  1.4 0.2 convert_reduce_fusion
  1.7 0.0 copy-start
  1.7 0.1 select_reduce_fusion
  1.8 0.6 broadcast_add_fusion.tok_ref
  2.4 0.0 copy-done
  2.4 186.1 %layer.1 = (bf16[3,16,4096]{2,1,0:T(8,128)(2,1)}, f32[2,16]{1,0:T(2,128)}, bf16[1,4096,768]{2,1,0:T(8,128)(2,1)}, bf16[1,4096,768]{2,1,0:T(8,128)(2,1)}, bf16[1,768,4096]{2,1,0:T(8,128)(2,1)}) custom-call(s32[192]{0:T(256)} %broadcast_add_fusion.tok_ref, s32[128]{0:T(128)} %copy-done, f32[8,16]{1,0:T(8,128)} %bitcast.4, bf16[3,128,512]{2,1,0:T(8,128)(2,1)} %q_hbm.1, ...), custom_call_target="tpu_custom_call" | custom-call | tf_op jit(solution)/shard_map/layer/pallas_call | solution.py:564
  188.5 1.8 copy.15
  190.3 1.2 copy.16
  (1 shorter events, 0.0 us)
Async XLA Ops:
  1.7 0.7 copy-start

commit v8 on v7

--- a/solution.py
+++ b/solution.py
@@ -68,6 +68,7 @@
     own,
     y_send,
     y_recv,
+    keep,
     send,
     recv,
     back,
@@ -282,35 +283,52 @@
             copy.start()
             sib_copies.append(copy)
         own_rows = block_rows(core)
-        y_copies = []
+
+        def y_copy(n, kind):
+            up = kind in (0, 2, 3)
+            device = y_peer(1) if up else y_peer(3)
+            return remote(y_send.at[n, kind], y_recv.at[n, kind], ys_send.at[n, kind], ys_recv.at[n, kind], device)
+
         for n in range(4):
             lanes = slice(n * 1024, (n + 1) * 1024)
             product = dot(own_rows, wo[:, lanes])
             sib_copies[n].wait_recv()
             both = product + sib_recv[n].astype(F32)
             own[:, lanes] = both[:48]
-            for d in order:
-                y_send[n, d - 1] = both[48 * d : 48 * (d + 1)].astype(BF)
-                copy = remote(
-                    y_send.at[n, d - 1], y_recv.at[n, d - 1], ys_send.at[n, d - 1], ys_recv.at[n, d - 1], y_peer(d)
-                )
-                copy.start()
-                y_copies.append(copy)
+            y_send[n, 0] = both[96:144, :512].astype(BF)
+            y_copy(n, 0).start()
+            y_send[n, 1] = both[96:144, 512:].astype(BF)
+            y_copy(n, 1).start()
+            y_send[n, 3] = both[48:96, 512:].astype(BF)
+            y_copy(n, 3).start()
+            y_send[n, 4] = both[144:, :512].astype(BF)
+            y_copy(n, 4).start()
+            keep[n, 0] = both[48:96, :512]
+            keep[n, 1] = both[144:, 512:]
+        for n in range(4):
+            for side in (0, 1):
+                y_copy(n, side).wait_recv()
+                kind = 2 + 3 * side
+                y_send[n, kind] = (keep[n, side] + y_recv[n, side].astype(F32)).astype(BF)
+                y_copy(n, kind).start()
         for part in range(4):
             weight_copy(1, part).start()
         for part in range(4):
             weight_copy(2, part).start()
         res_in.wait()
         for n in range(4):
-            for d in (1, 2, 3):
-                y_copies[n * 3 + order.index(d)].wait_recv()
-            lanes = slice(n * 1024, (n + 1) * 1024)
-            part = own[:, lanes]
-            for d in (1, 2, 3):
-                part += y_recv[n, d - 1].astype(F32)
-            for s in range(3):
-                summed_ref[s, :, lanes] = part[16 * s : 16 * (s + 1)] + res_ref[s, :, lanes].astype(F32)
-        for copy in kv_sent + sib_copies + y_copies:
+            for kind in (3, 4, 2, 5):
+                y_copy(n, kind).wait_recv()
+            for half in (0, 1):
+                first = n * 1024 + half * 512
+                lanes = slice(first, first + 512)
+                part = own[:, lanes] + y_recv[n, 2 + half].astype(F32) + y_recv[n, 4 + half].astype(F32)
+                for s in range(3):
+                    summed_ref[s, :, lanes] = part[16 * s : 16 * (s + 1)] + res_ref[s, :, lanes].astype(F32)
+        for n in range(4):
+            for kind in range(6):
+                y_copy(n, kind).wait_send()
+        for copy in kv_sent + sib_copies:
             copy.wait_send()
 
     pl.run_scoped(
@@ -583,8 +601,9 @@
             pltpu.VMEM((4, 192, 1024), BF),
             pltpu.VMEM((4, 192, 1024), BF),
             pltpu.VMEM((48, D), F32),
-            pltpu.VMEM((4, 3, 48, 1024), BF),
-            pltpu.VMEM((4, 3, 48, 1024), BF),
+            pltpu.VMEM((4, 6, 48, 512), BF),
+            pltpu.VMEM((4, 6, 48, 512), BF),
+            pltpu.VMEM((4, 2, 48, 512), F32),
             pltpu.VMEM(tiles, BF),
             pltpu.VMEM(tiles, BF),
             pltpu.VMEM(tiles, BF),
@@ -596,8 +615,8 @@
             dma((2, SEQ, 2)),
             dma((4,)),
             dma((4,)),
-            dma((4, 3)),
-            dma((4, 3)),
+            dma((4, 6)),
+            dma((4, 6)),
             dma((CHIPS,)),
             dma((CHIPS,)),
             dma((CHIPS,)),

time: 192 us -> 194 us (1.010)
  the two profiles are of different devices: /device:TPU:4 before, /device:TPU:16 now
where the time goes in v8:
time: 194 us; the launch traced here: 193 us
  Pallas kernels  188 us (97%)
  local copies, waits for them, and re-layouts  3.77 us (2%)
    pallas_call x1, Pallas kernels, layer(): pl.pallas_call(layer_kernel, out_shape=(jax.ShapeDtypeStruct((3, TOK, D),...  188 us

profile of v8, /device:TPU:16, one launch (start us, length us, event | category | flops | bytes accessed | tf_op | source)
XLA Modules:
  0.0 193.1 jit_solution(16421781810085129357)
XLA Ops:
  0.7 0.8 reshape.156
  1.4 0.2 convert_reduce_fusion
  1.7 0.0 copy-start
  1.7 0.1 select_reduce_fusion
  1.8 0.6 broadcast_add_fusion.tok_ref
  2.4 0.0 copy-done
  2.4 187.8 %layer.1 = (bf16[3,16,4096]{2,1,0:T(8,128)(2,1)}, f32[2,16]{1,0:T(2,128)}, bf16[1,4096,768]{2,1,0:T(8,128)(2,1)}, bf16[1,4096,768]{2,1,0:T(8,128)(2,1)}, bf16[1,768,4096]{2,1,0:T(8,128)(2,1)}) custom-call(s32[192]{0:T(256)} %broadcast_add_fusion.tok_ref, s32[128]{0:T(128)} %copy-done, f32[8,16]{1,0:T(8,128)} %bitcast.4, bf16[3,128,512]{2,1,0:T(8,128)(2,1)} %q_hbm.1, ...), custom_call_target="tpu_custom_call" | custom-call | tf_op jit(solution)/shard_map/layer/pallas_call | solution.py:582
  190.1 1.8 copy.15
  191.9 1.2 copy.16
  (1 shorter events, 0.0 us)
Async XLA Ops:
  1.7 0.7 copy-start

commit v9 on v7

--- a/solution.py
+++ b/solution.py
@@ -26,7 +26,7 @@
 HALF = 32
 ROWS = HALF * VECS
 FT = 256
-WINDOW = 24
+WINDOW = 14
 NT = 512
 
 

time: 192 us -> 200 us (1.042)
  the two profiles are of different devices: /device:TPU:4 before, /device:TPU:2 now
where the time goes in v9:
time: 200 us
  Pallas kernels  194 us (97%)
  local copies, waits for them, and re-layouts  3.77 us (2%)
    pallas_call x1, Pallas kernels, layer(): pl.pallas_call(layer_kernel, out_shape=(jax.ShapeDtypeStruct((3, TOK, D),...  194 us

profile of v9, /device:TPU:2, one launch (start us, length us, event | category | flops | bytes accessed | tf_op | source)
XLA Modules:
  0.0 199.8 jit_solution(8732266542172650723)
XLA Ops:
  0.7 0.8 reshape.156
  1.4 0.2 convert_reduce_fusion
  1.7 0.0 copy-start
  1.7 0.1 select_reduce_fusion
  1.8 0.6 broadcast_add_fusion.tok_ref
  2.4 0.0 copy-done
  2.4 194.4 %layer.1 = (bf16[3,16,4096]{2,1,0:T(8,128)(2,1)}, f32[2,16]{1,0:T(2,128)}, bf16[1,4096,768]{2,1,0:T(8,128)(2,1)}, bf16[1,4096,768]{2,1,0:T(8,128)(2,1)}, bf16[1,768,4096]{2,1,0:T(8,128)(2,1)}) custom-call(s32[192]{0:T(256)} %broadcast_add_fusion.tok_ref, s32[128]{0:T(128)} %copy-done, f32[8,16]{1,0:T(8,128)} %bitcast.4, bf16[3,128,512]{2,1,0:T(8,128)(2,1)} %q_hbm.1, ...), custom_call_target="tpu_custom_call" | custom-call | tf_op jit(solution)/shard_map/layer/pallas_call | solution.py:564
  196.7 1.8 copy.15
  198.5 1.2 copy.16
  (1 shorter events, 0.0 us)
Async XLA Ops:
  1.7 0.7 copy-start
